TPU v7x, 32 devices: a whole 2x2x4 slice. The times are simulated.
32 devices in a mesh: gx: 2 (over x), gy: 4 (over z), gz: 4 (over y, core).
Axes of the slice: x: 2, y: 2, z: 4, core: 2. Of those that a mesh axis runs over, the one named last changes fastest.
Arguments:
- field: bfloat16 [32, 6, 32, 512], P(None, 'gx', 'gy', 'gz'), may hold values from -6 to 6
- cotangent: bfloat16 [32, 6, 32, 512], P(None, 'gx', 'gy', 'gz'), may hold values from -6 to 6
- cosmology: float32 [2], replicated, may hold values from -1 to 1
- lift_weight: float32 [2, 256], replicated, may hold values from -4 to 4
- lift_bias: float32 [256], replicated, may hold values from -3 to 3
- style_weight: float32 [256, 32], replicated, may hold values from -0.375 to 0.375
- style_bias: float32 [32], replicated, may hold values from -2 to 2
- kernel: float32 [32, 32, 3, 3, 3], replicated, may hold values from -0.21875 to 0.21875
- offset: float32 [32], replicated, may hold values from -3 to 3
Outputs:
- grad_field: bfloat16 [32, 6, 32, 512], P(None, 'gx', 'gy', 'gz')
- grad_kernel: float32 [32, 32, 3, 3, 3], replicated
- grad_offset: float32 [32], replicated
- grad_lift: float32 [2, 256], replicated
- grad_liftbias: float32 [256], replicated
- grad_style: float32 [256, 32], replicated
- grad_stylebias: float32 [32], replicated
All inputs are finite; a program needn't handle non-finite values.
Results may differ from a plain program's by a relative error of at most 0.013.
Values may be sent and summed in bfloat16 or wider, within the bound.
A program may use at most 64 MiB of HBM per device.

v0:
```python
import functools

import jax
import jax.numpy as jnp
from jax import lax
from jax.experimental import pallas as pl
from jax.experimental.pallas import tpu as pltpu
from jax.sharding import PartitionSpec as P

demod_eps = 1e-06
clip_eps = 1e-06
MESH = pl.DeviceIdType.MESH
SIDES = tuple((dx, dy) for dx in (-1, 0, 1) for dy in (-1, 0, 1) if (dx, dy) != (0, 0))


def silu_slope(values):
    logistic = 1.0 / (1.0 + jnp.exp(-values))
    return logistic * (1.0 + values * (1.0 - logistic))


def kernel_body(
    sizes,
    field, cotangent, cosmology, lift_weight, lift_bias, style_t, style_bias, kernel, offset,
    grad, grad_kernel, grad_offset, grad_lift, grad_liftbias, grad_style_t, grad_stylebias,
    field_ext, up_ext, field_taps, up_taps, edge_out, edge_in, w_fwd, w_bwd, packed,
    share, from_z, part_z, from_y, part_y, from_x, total,
    xy_send, xy_recv, z_send, z_recv, rz_send, rz_recv, ry_send, ry_recv, rx_send, rx_recv,
    gy_send, gy_recv, gz_send, gz_recv,
):
    nx, ny, nz = sizes
    C, CX, CY, CZ = field.shape[2], field.shape[0], field.shape[1], field.shape[3]
    EY = CY + 2
    taps = kernel.shape[0]
    per = CZ // C
    tiles = (taps + per) // per
    me_x, me_y, me_z = (lax.axis_index("gx"), lax.axis_index("gy"), lax.axis_index("gz"))

    def at(dx=0, dy=0, dz=0):
        return (
            lax.rem(me_x + (dx + nx), nx) if dx else me_x,
            lax.rem(me_y + (dy + ny), ny) if dy else me_y,
            lax.rem(me_z + (dz + nz), nz) if dz else me_z,
        )

    partners = [at(dx, dy) for dx, dy in SIDES]
    partners += [at(dz=k) for k in range(1, nz)]
    partners += [at(dy=k) for k in range(1, ny)]
    partners += [at(dx=k) for k in range(1, nx)]
    barrier = pltpu.get_barrier_semaphore()
    for partner in partners:
        pl.semaphore_signal(barrier, inc=1, device_id=partner, device_id_type=MESH)

    def remote(src, dst, send, recv, device):
        return pltpu.make_async_remote_copy(
            src_ref=src, dst_ref=dst, send_sem=send, recv_sem=recv, device_id=device,
            device_id_type=MESH,
        )

    def span(step, count, first):
        if step == 0:
            return pl.ds(first, count), pl.ds(1, count)
        if step > 0:
            return pl.ds(first + count - 1, 1), pl.ds(0, 1)
        return pl.ds(first, 1), pl.ds(count + 1, 1)

    def side_copies(which, source, first, ext):
        copies = []
        for at_side, (dx, dy) in enumerate(SIDES):
            sx, tx = span(dx, CX, first)
            sy, ty = span(dy, CY, first)
            copies.append(
                remote(source.at[sx, sy], ext.at[tx, ty], xy_send.at[which, at_side],
                       xy_recv.at[which, at_side], at(dx, dy))
            )
        return copies

    lanes = lax.broadcasted_iota(jnp.int32, (C, CZ), 1)
    group = lax.div(lanes, 2)

    def edge_copies(which):
        return [
            remote(edge_out.at[which], edge_in.at[which, 0], z_send.at[which, 0],
                   z_recv.at[which, 0], at(dz=1)),
            remote(edge_out.at[which], edge_in.at[which, 1], z_send.at[which, 1],
                   z_recv.at[which, 1], at(dz=-1)),
        ]

    def pack_edges(which, ext):
        def plane(p, edges):
            for y in range(EY):
                row = p * EY + y
                rolled = pltpu.roll(ext[p, y].astype(jnp.float32), 1 + 2 * row, 1)
                edges = jnp.where(group == row, rolled, edges)
            return edges

        edges = lax.fori_loop(0, CX + 2, plane, jnp.zeros((C, CZ), jnp.float32))
        edge_out[which] = edges.astype(jnp.bfloat16)

    def build_taps(which, ext, out):
        before = edge_in[which, 0].astype(jnp.float32)
        after = edge_in[which, 1].astype(jnp.float32)

        def plane(p, carry):
            for y in range(EY):
                row = p * EY + y
                mid = ext[p, y]
                wide = mid.astype(jnp.float32)
                low = jnp.where(lanes == 0, pltpu.roll(before, lax.rem(CZ - 2 * row, CZ), 1),
                                pltpu.roll(wide, 1, 1))
                high = jnp.where(lanes == CZ - 1, pltpu.roll(after, CZ - 2 - 2 * row, 1),
                                 pltpu.roll(wide, CZ - 1, 1))
                out[p, y, 0:C] = low.astype(jnp.bfloat16)
                out[p, y, C : 2 * C] = mid
                out[p, y, 2 * C : 3 * C] = high.astype(jnp.bfloat16)
            return carry

        lax.fori_loop(0, CX + 2, plane, 0)

    def columns(source, x, y):
        both = []
        for k in range(2):
            planes = [source[x + a, pl.ds(y + k, 3)].reshape(9 * C, CZ) for a in range(3)]
            both.append(jnp.concatenate(planes, axis=0))
        return jnp.concatenate(both, axis=1)

    field_ext[1 : CX + 1, 1 : CY + 1] = field[...]
    pl.semaphore_wait(barrier, len(partners))
    field_sides = side_copies(0, field, 0, field_ext)
    for copy in field_sides:
        copy.start()

    eye = lax.broadcasted_iota(jnp.int32, (C, C), 0) == lax.broadcasted_iota(jnp.int32, (C, C), 1)

    def to_row(column):
        return jnp.sum(jnp.where(eye, column, 0.0), axis=0, keepdims=True)

    def to_column(row):
        return jnp.sum(jnp.where(eye, row, 0.0), axis=1, keepdims=True)

    lifted = lift_bias[...]
    for k in range(lift_weight.shape[0]):
        lifted = lifted + cosmology[0:1, k : k + 1] * lift_weight[k : k + 1, :]
    hidden = lifted / (1.0 + jnp.exp(-lifted))
    styles_column = (
        jnp.sum(style_t[...] * hidden, axis=1, keepdims=True) + to_column(style_bias[...]) + 1.0
    )
    styles = to_row(styles_column)
    styles_wide = jnp.concatenate([styles] * per, axis=1)
    squares = jnp.zeros((C, CZ), jnp.float32)
    for j in range(tiles):
        members = [
            kernel[per * j + k] if per * j + k < taps else jnp.zeros((C, C), jnp.float32)
            for k in range(per)
        ]
        tile = jnp.concatenate(members, axis=1)
        packed[j] = tile
        modded = tile * styles_wide
        squares = squares + modded * modded
    inv_norm = lax.rsqrt(jnp.sum(squares, axis=1, keepdims=True) + demod_eps)
    turned = []
    for j in range(tiles):
        scaled = packed[j] * styles_wide * inv_norm
        w_fwd[:, j * CZ : (j + 1) * CZ] = scaled.astype(jnp.bfloat16)
        flat = scaled.T
        turned += [flat[k * C : (k + 1) * C] for k in range(per)]
    turned = turned[:taps][::-1] + [jnp.zeros((C, C), jnp.float32)] * (tiles * per - taps)
    for j in range(tiles):
        w_bwd[:, j * CZ : (j + 1) * CZ] = jnp.concatenate(
            turned[per * j : per * (j + 1)], axis=1
        ).astype(jnp.bfloat16)
    offset_column = to_column(offset[...])

    for copy in field_sides:
        copy.wait()
    pack_edges(0, field_ext)
    field_edges = edge_copies(0)
    for copy in field_edges:
        copy.start()
    for copy in field_edges:
        copy.wait()
    build_taps(0, field_ext, field_taps)

    depth = taps * C

    def forward(x, carry):
        for y in range(0, CY, 2):
            preact = jnp.dot(w_fwd[:, :depth], columns(field_taps, x, y),
                             preferred_element_type=jnp.float32) + offset_column
            cot = jnp.concatenate([cotangent[x, y], cotangent[x, y + 1]], axis=1)
            upstream = (cot.astype(jnp.float32) * silu_slope(preact)).astype(jnp.bfloat16)
            up_ext[x + 1, y + 1] = upstream[:, :CZ]
            up_ext[x + 1, y + 2] = upstream[:, CZ:]
        return carry

    lax.fori_loop(0, CX, forward, 0)
    up_sides = side_copies(1, up_ext, 1, up_ext)
    for copy in up_sides:
        copy.start()

    def weigh(x, carry):
        sums, offsets = carry
        for y in range(0, CY, 2):
            upstream = jnp.concatenate([up_ext[x + 1, y + 1], up_ext[x + 1, y + 2]], axis=1)
            sums = sums + lax.dot_general(
                upstream, columns(field_taps, x, y), (((1,), (1,)), ((), ())),
                preferred_element_type=jnp.float32,
            )
            wide = upstream.astype(jnp.float32)
            offsets = offsets + wide[:, :CZ] + wide[:, CZ:]
        return (sums, offsets)

    sums, offsets = lax.fori_loop(
        0, CX, weigh,
        (jnp.zeros((C, depth), jnp.float32), jnp.zeros((C, CZ), jnp.float32)),
    )
    offset_sum = jnp.sum(offsets, axis=1, keepdims=True)
    rows = C * tiles
    share[...] = jnp.zeros_like(share)
    for j in range(tiles):
        if (j + 1) * CZ <= depth:
            share[j * C : (j + 1) * C] = sums[:, j * CZ : (j + 1) * CZ]
        else:
            used = depth - j * CZ
            share[j * C : (j + 1) * C] = jnp.concatenate(
                [sums[:, j * CZ : depth], jnp.broadcast_to(offset_sum, (C, CZ - used))], axis=1
            )

    rows_z = share.shape[0] // nz
    rows_y = rows_z // ny

    def rows_at(base, count):
        return pl.ds(pl.multiple_of(base, 8), count)

    reduce_z = []
    for k in range(1, nz):
        there = at(dz=k)
        reduce_z.append(remote(share.at[rows_at(there[2] * rows_z, rows_z)], from_z.at[k - 1],
                               rz_send.at[k - 1], rz_recv.at[k - 1], there))
    for copy in reduce_z:
        copy.start()

    for copy in up_sides:
        copy.wait()
    pack_edges(1, up_ext)
    up_edges = edge_copies(1)
    for copy in up_edges:
        copy.start()

    for copy in reduce_z:
        copy.wait()
    mine = share[rows_at(me_z * rows_z, rows_z), :]
    for k in range(1, nz):
        mine = mine + from_z[k - 1]
    part_z[...] = mine
    reduce_y = []
    for k in range(1, ny):
        there = at(dy=k)
        reduce_y.append(remote(part_z.at[rows_at(there[1] * rows_y, rows_y)], from_y.at[k - 1],
                               ry_send.at[k - 1], ry_recv.at[k - 1], there))
    for copy in reduce_y:
        copy.start()

    for copy in up_edges:
        copy.wait()
    build_taps(1, up_ext, up_taps)

    for copy in reduce_y:
        copy.wait()
    mine = part_z[rows_at(me_y * rows_y, rows_y), :]
    for k in range(1, ny):
        mine = mine + from_y[k - 1]
    part_y[...] = mine
    from_x[me_x] = mine
    reduce_x = [
        remote(part_y, from_x.at[me_x], rx_send.at[k - 1], rx_recv.at[k - 1], at(dx=k))
        for k in range(1, nx)
    ]
    for copy in reduce_x:
        copy.start()

    def backward(x, carry):
        for y in range(0, CY, 2):
            result = jnp.dot(w_bwd[:, :depth], columns(up_taps, x, y),
                             preferred_element_type=jnp.float32).astype(jnp.bfloat16)
            grad[x, y] = result[:, :CZ]
            grad[x, y + 1] = result[:, CZ:]
        return carry

    lax.fori_loop(0, 1, backward, 0)

    for copy in reduce_x:
        copy.wait()
    mine = from_x[0]
    for k in range(1, nx):
        mine = mine + from_x[k]
    own_y = rows_at(me_z * rows_z + me_y * rows_y, rows_y)
    total[own_y, :] = mine
    gather_y = [
        remote(total.at[own_y], total.at[own_y], gy_send.at[k - 1], gy_recv.at[k - 1], at(dy=k))
        for k in range(1, ny)
    ]
    for copy in gather_y:
        copy.start()
    lax.fori_loop(1, 2, backward, 0)
    for copy in gather_y:
        copy.wait()
    own_z = rows_at(me_z * rows_z, rows_z)
    gather_z = [
        remote(total.at[own_z], total.at[own_z], gz_send.at[k - 1], gz_recv.at[k - 1], at(dz=k))
        for k in range(1, nz)
    ]
    for copy in gather_z:
        copy.start()
    lax.fori_loop(2, CX, backward, 0)
    for copy in gather_z:
        copy.wait()

    last = taps - per * (tiles - 1)
    projected = jnp.zeros((C, CZ), jnp.float32)
    sum_tiles, modded_tiles = [], []
    for j in range(tiles):
        tile = total[j * C : (j + 1) * C, :]
        if j == tiles - 1:
            offset_row = to_row(tile[:, last * C : last * C + 1])
            tile = jnp.where(lanes < last * C, tile, 0.0)
        modded = packed[j] * styles_wide
        projected = projected + tile * modded
        sum_tiles.append(tile)
        modded_tiles.append(modded)
    projected = jnp.sum(projected, axis=1, keepdims=True)
    scale = inv_norm * inv_norm * projected
    raws = []
    square = jnp.zeros((C, CZ), jnp.float32)
    along = jnp.zeros((C, CZ), jnp.float32)
    for j in range(tiles):
        mod_grad = inv_norm * (sum_tiles[j] - modded_tiles[j] * scale)
        raw = mod_grad * styles_wide
        along = along + mod_grad * packed[j]
        square = square + raw * raw
        raws.append(raw)
    along = jnp.sum(along, axis=0, keepdims=True)
    styles_grad = along[:, 0:C]
    for k in range(1, per):
        styles_grad = styles_grad + along[:, k * C : (k + 1) * C]
    styles_grad_column = to_column(styles_grad)
    hidden_grad = jnp.sum(style_t[...] * styles_grad_column, axis=0, keepdims=True)
    lifted_grad = hidden_grad * silu_slope(lifted)
    style_raw = styles_grad_column * hidden
    lift_raws = [
        cosmology[0:1, k : k + 1] * lifted_grad for k in range(lift_weight.shape[0])
    ]

    def sum_all(values):
        return jnp.sum(jnp.sum(values, axis=1, keepdims=True), axis=0, keepdims=True)

    square_sum = sum_all(square)
    for member in [offset_row, lifted_grad, style_raw, styles_grad] + lift_raws:
        square_sum = square_sum + sum_all(member * member)
    entries = taps * C * C + 2 * C + (1 + lift_weight.shape[0] + C) * lifted.shape[1]
    factor = jnp.minimum(1.0, lax.rsqrt(square_sum / entries + clip_eps))
    for j in range(tiles):
        scaled_raw = raws[j] * factor
        for k in range(per):
            if per * j + k < taps:
                grad_kernel[per * j + k] = scaled_raw[:, k * C : (k + 1) * C]
    grad_offset[...] = offset_row * factor
    for k in range(lift_weight.shape[0]):
        grad_lift[k : k + 1, :] = lift_raws[k] * factor
    grad_liftbias[...] = lifted_grad * factor
    grad_style_t[...] = style_raw * factor
    grad_stylebias[...] = styles_grad * factor


def body(
    sizes, field, cotangent, cosmology, lift_weight, lift_bias, style_weight, style_bias, kernel,
    offset,
):
    nx, ny, nz = sizes
    C, CX, CY, CZ = field.shape
    HID = lift_bias.shape[0]
    taps = kernel.shape[2] * kernel.shape[3] * kernel.shape[4]
    per = CZ // C
    tiles = (taps + per) // per
    unit = nz * ny * 8
    rows = -(-tiles * C // unit) * unit
    f32, bf16 = jnp.float32, jnp.bfloat16
    dma = pltpu.SemaphoreType.DMA
    vmem = pl.BlockSpec(memory_space=pltpu.VMEM)
    results = pl.pallas_call(
        functools.partial(kernel_body, sizes),
        out_shape=[
            jax.ShapeDtypeStruct((CX, CY, C, CZ), bf16),
            jax.ShapeDtypeStruct((taps, C, C), f32),
            jax.ShapeDtypeStruct((1, C), f32),
            jax.ShapeDtypeStruct(lift_weight.shape, f32),
            jax.ShapeDtypeStruct((1, HID), f32),
            jax.ShapeDtypeStruct((C, HID), f32),
            jax.ShapeDtypeStruct((1, C), f32),
        ],
        in_specs=[vmem] * 9,
        out_specs=[vmem] * 7,
        scratch_shapes=[
            pltpu.VMEM((CX + 2, CY + 2, C, CZ), bf16),
            pltpu.VMEM((CX + 2, CY + 2, C, CZ), bf16),
            pltpu.VMEM((CX + 2, CY + 2, 3 * C, CZ), bf16),
            pltpu.VMEM((CX + 2, CY + 2, 3 * C, CZ), bf16),
            pltpu.VMEM((2, C, CZ), bf16),
            pltpu.VMEM((2, 2, C, CZ), bf16),
            pltpu.VMEM((C, tiles * CZ), bf16),
            pltpu.VMEM((C, tiles * CZ), bf16),
            pltpu.VMEM((tiles, C, CZ), f32),
            pltpu.VMEM((rows, CZ), f32),
            pltpu.VMEM((nz - 1, rows // nz, CZ), f32),
            pltpu.VMEM((rows // nz, CZ), f32),
            pltpu.VMEM((ny - 1, rows // nz // ny, CZ), f32),
            pltpu.VMEM((rows // nz // ny, CZ), f32),
            pltpu.VMEM((nx, rows // nz // ny, CZ), f32),
            pltpu.VMEM((rows, CZ), f32),
            dma((2, 8)), dma((2, 8)), dma((2, 2)), dma((2, 2)),
            dma((nz - 1,)), dma((nz - 1,)), dma((ny - 1,)), dma((ny - 1,)),
            dma((nx - 1,)), dma((nx - 1,)), dma((ny - 1,)), dma((ny - 1,)),
            dma((nz - 1,)), dma((nz - 1,)),
        ],
        compiler_params=pltpu.CompilerParams(
            collective_id=0, has_side_effects=True, vmem_limit_bytes=32 * 1024 * 1024
        ),
    )(
        jnp.transpose(field, (1, 2, 0, 3)),
        jnp.transpose(cotangent, (1, 2, 0, 3)),
        cosmology[None],
        lift_weight,
        lift_bias[None],
        style_weight.T,
        style_bias[None],
        jnp.transpose(kernel, (2, 3, 4, 0, 1)).reshape(taps, C, C),
        offset[None],
    )
    grad, grad_kernel, grad_offset, grad_lift, grad_liftbias, grad_style_t, grad_stylebias = results
    return (
        jnp.transpose(grad, (2, 0, 1, 3)),
        jnp.transpose(grad_kernel.reshape(kernel.shape[2:] + (C, C)), (3, 4, 0, 1, 2)),
        grad_offset[0],
        grad_lift,
        grad_liftbias[0],
        grad_style_t.T,
        grad_stylebias[0],
    )


def solution(mesh):
    sizes = (mesh.shape["gx"], mesh.shape["gy"], mesh.shape["gz"])
    placed = P(None, "gx", "gy", "gz")
    return jax.shard_map(
        functools.partial(body, sizes),
        mesh=mesh,
        in_specs=(placed, placed, P(), P(), P(), P(), P(), P(), P()),
        out_specs=(placed, P(), P(), P(), P(), P(), P()),
        check_vma=False,
    )
```

profile of v0, /device:TPU:0, one launch (start us, length us, event | category | flops | bytes accessed | tf_op | source)
XLA Modules:
  0.0 42.2 jit_solution(10220234627530801123)
XLA Ops:
  0.6 0.0 copy-start
  0.6 0.0 copy-start.1
  0.7 0.0 copy-start.5
  0.7 0.0 copy-start.6
  0.7 1.1 %copy_bitcast_fusion = (bf16[3,8,32,128]{3,2,1,0:T(8,128)(2,1)S(1)}, bf16[3,8,32,128]{3,2,1,0:T(8,128)(2,1)S(1)}) fusion(bf16[32,3,8,128]{3,2,1,0:T(8,128)(2,1)} %param.10, bf16[32,3,8,128]{3,2,1,0:T(8,128)(2,1)} %param.9), kind=kLoop, calls=%fused_computation | loop fusion | bytes 786432 | tf_op jit(solution)/shard_map/transpose | solution.py:429
  1.8 0.0 copy-start.2
  1.8 0.0 copy-start.3
  1.8 0.0 copy-start.4
  1.8 0.0 copy-done
  1.9 0.0 copy-done.1
  1.9 0.0 copy-done.5
  1.9 0.0 copy-done.6
  1.9 0.6 %copy-done.2 = f32[2,256]{1,0:T(2,128)S(1)} copy-done((f32[2,256]{1,0:T(2,128)S(1)}, f32[2,256]{1,0:T(2,128)}, u32[]{:S(2)}) %copy-start.2) | copy-done | bytes 2072
  2.5 0.0 copy-done.3
  2.5 0.0 copy-done.4
  2.5 35.4 %shard_map.144 = (bf16[3,8,32,128]{3,2,1,0:T(8,128)(2,1)S(1)}, f32[27,32,32]{2,1,0:T(8,128)S(1)}, f32[1,32]{1,0:T(1,128)S(1)}, f32[2,256]{1,0:T(2,128)S(1)}, f32...) custom-call(bf16[3,8,32,128]{3,2,1,0:T(8,128)(2,1)S(1)} %get-tuple-element.29.field, ...), custom_call_target="tpu_custom_call" | custom-call | tf_op jit(solution)/shard_map/pallas_call | solution.py:389
  37.9 0.8 %copy.18 = bf16[32,3,8,128]{3,2,1,0:T(8,128)(2,1)} copy(bf16[32,3,8,128]{3,0,2,1:T(8,128)(2,1)S(1)} %bitcast.22) | data formatting | bytes 393216
  38.6 0.8 %copy.27 = f32[32,32,3,3,3]{1,0,4,3,2:T(8,128)} copy(f32[32,32,3,3,3]{1,0,4,3,2:T(8,128)S(1)} %bitcast.21) | data formatting | bytes 221184
  39.4 0.5 %copy.28 = f32[32]{0:T(128)} copy(f32[32]{0:T(128)S(1)} %bitcast.31) | data formatting | bytes 256
  39.9 0.6 %copy.29 = f32[2,256]{1,0:T(2,128)} copy(f32[2,256]{1,0:T(2,128)S(1)} %get-tuple-element.40) | data formatting | bytes 4096
  40.5 0.6 %copy.30 = f32[256]{0:T(256)} copy(f32[256]{0:T(256)S(1)} %bitcast.26) | data formatting | bytes 2048
  41.0 0.6 %copy.31 = f32[256,32]{0,1:T(8,128)} copy(f32[256,32]{0,1:T(8,128)S(1)} %bitcast.24) | data formatting | bytes 65536
  41.7 0.5 %copy.32 = f32[32]{0:T(128)} copy(f32[32]{0:T(128)S(1)} %bitcast.30) | data formatting | bytes 256
Async XLA Ops:
  0.6 1.2 %copy-start = (f32[32,32,3,3,3]{1,0,4,3,2:T(8,128)S(1)}, f32[32,32,3,3,3]{1,0,4,3,2:T(8,128)}, u32[]{:S(2)}) copy-start(f32[32,32,3,3,3]{1,0,4,3,2:T(8,128)} %param.16) | copy-start | bytes 331780
  0.6 1.2 %copy-start.1 = (f32[256,32]{0,1:T(8,128)S(1)}, f32[256,32]{0,1:T(8,128)}, u32[]{:S(2)}) copy-start(f32[256,32]{0,1:T(8,128)} %param.14) | copy-start | bytes 98308
  0.7 1.2 %copy-start.5 = (f32[32]{0:T(128)S(1)}, f32[32]{0:T(128)}, u32[]{:S(2)}) copy-start(f32[32]{0:T(128)} %param.15) | copy-start | bytes 388
  0.7 1.2 %copy-start.6 = (f32[32]{0:T(128)S(1)}, f32[32]{0:T(128)}, u32[]{:S(2)}) copy-start(f32[32]{0:T(128)} %param.17) | copy-start | bytes 388
  1.8 0.7 %copy-start.2 = (f32[2,256]{1,0:T(2,128)S(1)}, f32[2,256]{1,0:T(2,128)}, u32[]{:S(2)}) copy-start(f32[2,256]{1,0:T(2,128)} %lift_weight.1) | copy-start | bytes 6148
  1.8 0.7 %copy-start.3 = (f32[256]{0:T(256)S(1)}, f32[256]{0:T(256)}, u32[]{:S(2)}) copy-start(f32[256]{0:T(256)} %param.13) | copy-start | bytes 3076
  1.8 0.7 %copy-start.4 = (f32[2]{0:T(128)S(1)}, f32[2]{0:T(128)}, u32[]{:S(2)}) copy-start(f32[2]{0:T(128)} %param.11) | copy-start | bytes 28
where the time goes:
time: 42.3 us; the launch traced here: 42.2 us
  Pallas kernels  35.4 us (84%)
  local copies, waits for them, and re-layouts  6.08 us (14%)
  between operations  0.74 us (2%)
    pallas_call x1, Pallas kernels, body(): pl.pallas_call(functools.partial(kernel_body, sizes), out_shape=[jax.Shap...  35.4 us
    unnamed x21, local copies, waits for them, and re-layouts  4.95 us
    transpose x1, local copies, waits for them, and re-layouts, body(): jnp.transpose(cotangent, (1, 2, 0, 3))  1.13 us

commit v1 on v0

--- a/solution.py
+++ b/solution.py
@@ -21,14 +21,13 @@
 def kernel_body(
     sizes,
     field, cotangent, cosmology, lift_weight, lift_bias, style_t, style_bias, kernel, offset,
-    grad, grad_kernel, grad_offset, grad_lift, grad_liftbias, grad_style_t, grad_stylebias,
-    field_ext, up_ext, field_taps, up_taps, edge_out, edge_in, w_fwd, w_bwd, packed,
-    share, from_z, part_z, from_y, part_y, from_x, total,
-    xy_send, xy_recv, z_send, z_recv, rz_send, rz_recv, ry_send, ry_recv, rx_send, rx_recv,
-    gy_send, gy_recv, gz_send, gz_recv,
+    grad, grad_packed, grad_rows, grad_style_t,
+    field_ext, up_ext, field_taps, up_taps, edge_out, edge_in, w_fwd, w_bwd, packed, cot, turned_back,
+    share, from_z, part_z, from_xy, total,
+    xy_send, xy_recv, z_send, z_recv, rz_send, rz_recv, rxy_send, rxy_recv, g_send, g_recv,
 ):
     nx, ny, nz = sizes
-    C, CX, CY, CZ = field.shape[2], field.shape[0], field.shape[1], field.shape[3]
+    C, CX, CY, CZ = field.shape
     EY = CY + 2
     taps = kernel.shape[0]
     per = CZ // C
@@ -43,9 +42,10 @@
         )
 
     partners = [at(dx, dy) for dx, dy in SIDES]
-    partners += [at(dz=k) for k in range(1, nz)]
-    partners += [at(dy=k) for k in range(1, ny)]
-    partners += [at(dx=k) for k in range(1, nx)]
+    plane_xy = [(dx, dy) for dx in range(nx) for dy in range(ny) if (dx, dy) != (0, 0)]
+    plane_yz = [(dy, dz) for dy in range(ny) for dz in range(nz) if (dy, dz) != (0, 0)]
+    partners += [at(dx, dy) for dx, dy in plane_xy]
+    partners += [at(0, dy, dz) for dy, dz in plane_yz]
     barrier = pltpu.get_barrier_semaphore()
     for partner in partners:
         pl.semaphore_signal(barrier, inc=1, device_id=partner, device_id_type=MESH)
@@ -123,9 +123,11 @@
             both.append(jnp.concatenate(planes, axis=0))
         return jnp.concatenate(both, axis=1)
 
-    field_ext[1 : CX + 1, 1 : CY + 1] = field[...]
+    for x in range(CX):
+        turned_x = jnp.swapaxes(field[:, x].astype(jnp.float32), 0, 1)
+        field_ext[x + 1, 1 : CY + 1] = turned_x.astype(jnp.bfloat16)
     pl.semaphore_wait(barrier, len(partners))
-    field_sides = side_copies(0, field, 0, field_ext)
+    field_sides = side_copies(0, field_ext, 1, field_ext)
     for copy in field_sides:
         copy.start()
 
@@ -169,6 +171,8 @@
             turned[per * j : per * (j + 1)], axis=1
         ).astype(jnp.bfloat16)
     offset_column = to_column(offset[...])
+    for x in range(CX):
+        cot[x] = jnp.swapaxes(cotangent[:, x].astype(jnp.float32), 0, 1)
 
     for copy in field_sides:
         copy.wait()
@@ -186,8 +190,8 @@
         for y in range(0, CY, 2):
             preact = jnp.dot(w_fwd[:, :depth], columns(field_taps, x, y),
                              preferred_element_type=jnp.float32) + offset_column
-            cot = jnp.concatenate([cotangent[x, y], cotangent[x, y + 1]], axis=1)
-            upstream = (cot.astype(jnp.float32) * silu_slope(preact)).astype(jnp.bfloat16)
+            above = jnp.concatenate([cot[x, y], cot[x, y + 1]], axis=1)
+            upstream = (above * silu_slope(preact)).astype(jnp.bfloat16)
             up_ext[x + 1, y + 1] = upstream[:, :CZ]
             up_ext[x + 1, y + 2] = upstream[:, CZ:]
         return carry
@@ -214,22 +218,23 @@
         (jnp.zeros((C, depth), jnp.float32), jnp.zeros((C, CZ), jnp.float32)),
     )
     offset_sum = jnp.sum(offsets, axis=1, keepdims=True)
-    rows = C * tiles
-    share[...] = jnp.zeros_like(share)
-    for j in range(tiles):
+    for j in range(share.shape[0] // C):
         if (j + 1) * CZ <= depth:
-            share[j * C : (j + 1) * C] = sums[:, j * CZ : (j + 1) * CZ]
-        else:
+            tile = sums[:, j * CZ : (j + 1) * CZ]
+        elif j < tiles:
             used = depth - j * CZ
-            share[j * C : (j + 1) * C] = jnp.concatenate(
+            tile = jnp.concatenate(
                 [sums[:, j * CZ : depth], jnp.broadcast_to(offset_sum, (C, CZ - used))], axis=1
             )
+        else:
+            tile = jnp.zeros((C, CZ), jnp.float32)
+        share[j * C : (j + 1) * C] = tile.astype(jnp.bfloat16)
 
     rows_z = share.shape[0] // nz
     rows_y = rows_z // ny
 
     def rows_at(base, count):
-        return pl.ds(pl.multiple_of(base, 8), count)
+        return pl.ds(pl.multiple_of(base, 16), count)
 
     reduce_z = []
     for k in range(1, nz):
@@ -248,78 +253,57 @@
 
     for copy in reduce_z:
         copy.wait()
-    mine = share[rows_at(me_z * rows_z, rows_z), :]
+    mine = share[rows_at(me_z * rows_z, rows_z), :].astype(jnp.float32)
     for k in range(1, nz):
-        mine = mine + from_z[k - 1]
-    part_z[...] = mine
-    reduce_y = []
-    for k in range(1, ny):
-        there = at(dy=k)
-        reduce_y.append(remote(part_z.at[rows_at(there[1] * rows_y, rows_y)], from_y.at[k - 1],
-                               ry_send.at[k - 1], ry_recv.at[k - 1], there))
-    for copy in reduce_y:
-        copy.start()
+        mine = mine + from_z[k - 1].astype(jnp.float32)
+    part_z[...] = mine.astype(jnp.bfloat16)
+    my_slot = me_x * ny + me_y
+    reduce_xy = []
+    for k, (dx, dy) in enumerate(plane_xy):
+        there = at(dx, dy)
+        reduce_xy.append(remote(part_z.at[rows_at(there[1] * rows_y, rows_y)], from_xy.at[my_slot],
+                                rxy_send.at[k], rxy_recv.at[k], there))
+    for copy in reduce_xy:
+        copy.start()
+    from_xy[my_slot] = part_z[rows_at(me_y * rows_y, rows_y), :]
 
     for copy in up_edges:
         copy.wait()
     build_taps(1, up_ext, up_taps)
-
-    for copy in reduce_y:
-        copy.wait()
-    mine = part_z[rows_at(me_y * rows_y, rows_y), :]
-    for k in range(1, ny):
-        mine = mine + from_y[k - 1]
-    part_y[...] = mine
-    from_x[me_x] = mine
-    reduce_x = [
-        remote(part_y, from_x.at[me_x], rx_send.at[k - 1], rx_recv.at[k - 1], at(dx=k))
-        for k in range(1, nx)
-    ]
-    for copy in reduce_x:
-        copy.start()
 
     def backward(x, carry):
         for y in range(0, CY, 2):
             result = jnp.dot(w_bwd[:, :depth], columns(up_taps, x, y),
-                             preferred_element_type=jnp.float32).astype(jnp.bfloat16)
-            grad[x, y] = result[:, :CZ]
-            grad[x, y + 1] = result[:, CZ:]
+                             preferred_element_type=jnp.float32)
+            turned_back[y] = result[:, :CZ]
+            turned_back[y + 1] = result[:, CZ:]
+        grad[:, x] = jnp.swapaxes(turned_back[...], 0, 1).astype(jnp.bfloat16)
         return carry
 
     lax.fori_loop(0, 1, backward, 0)
 
-    for copy in reduce_x:
-        copy.wait()
-    mine = from_x[0]
-    for k in range(1, nx):
-        mine = mine + from_x[k]
-    own_y = rows_at(me_z * rows_z + me_y * rows_y, rows_y)
-    total[own_y, :] = mine
-    gather_y = [
-        remote(total.at[own_y], total.at[own_y], gy_send.at[k - 1], gy_recv.at[k - 1], at(dy=k))
-        for k in range(1, ny)
+    for copy in reduce_xy:
+        copy.wait()
+    mine = from_xy[0].astype(jnp.float32)
+    for k in range(1, nx * ny):
+        mine = mine + from_xy[k].astype(jnp.float32)
+    own = rows_at(me_z * rows_z + me_y * rows_y, rows_y)
+    total[own, :] = mine.astype(jnp.bfloat16)
+    gather = [
+        remote(total.at[own], total.at[own], g_send.at[k], g_recv.at[k], at(0, dy, dz))
+        for k, (dy, dz) in enumerate(plane_yz)
     ]
-    for copy in gather_y:
-        copy.start()
-    lax.fori_loop(1, 2, backward, 0)
-    for copy in gather_y:
-        copy.wait()
-    own_z = rows_at(me_z * rows_z, rows_z)
-    gather_z = [
-        remote(total.at[own_z], total.at[own_z], gz_send.at[k - 1], gz_recv.at[k - 1], at(dz=k))
-        for k in range(1, nz)
-    ]
-    for copy in gather_z:
-        copy.start()
-    lax.fori_loop(2, CX, backward, 0)
-    for copy in gather_z:
+    for copy in gather:
+        copy.start()
+    lax.fori_loop(1, CX, backward, 0)
+    for copy in gather:
         copy.wait()
 
     last = taps - per * (tiles - 1)
     projected = jnp.zeros((C, CZ), jnp.float32)
     sum_tiles, modded_tiles = [], []
     for j in range(tiles):
-        tile = total[j * C : (j + 1) * C, :]
+        tile = total[j * C : (j + 1) * C, :].astype(jnp.float32)
         if j == tiles - 1:
             offset_row = to_row(tile[:, last * C : last * C + 1])
             tile = jnp.where(lanes < last * C, tile, 0.0)
@@ -359,16 +343,31 @@
     entries = taps * C * C + 2 * C + (1 + lift_weight.shape[0] + C) * lifted.shape[1]
     factor = jnp.minimum(1.0, lax.rsqrt(square_sum / entries + clip_eps))
     for j in range(tiles):
-        scaled_raw = raws[j] * factor
-        for k in range(per):
-            if per * j + k < taps:
-                grad_kernel[per * j + k] = scaled_raw[:, k * C : (k + 1) * C]
-    grad_offset[...] = offset_row * factor
+        grad_packed[j] = raws[j] * factor
+    grad_style_t[...] = style_raw * factor
+    wide = lifted.shape[1]
+    small = jnp.concatenate([offset_row, styles_grad], axis=1)
+    grad_rows[0:1, 0 : 2 * C] = small * factor
+    grad_rows[1:2, :] = lifted_grad * factor
     for k in range(lift_weight.shape[0]):
-        grad_lift[k : k + 1, :] = lift_raws[k] * factor
-    grad_liftbias[...] = lifted_grad * factor
-    grad_style_t[...] = style_raw * factor
-    grad_stylebias[...] = styles_grad * factor
+        grad_rows[k + 2 : k + 3, :] = lift_raws[k] * factor
+
+
+def hand_out(
+    grad_in, grad_packed, grad_rows, grad_style_in,
+    grad, grad_kernel, grad_offset, grad_lift, grad_liftbias, grad_style_t, grad_stylebias,
+):
+    C = grad_packed.shape[1]
+    per = grad_packed.shape[2] // C
+    grad[...] = grad_in[...]
+    for t in range(grad_kernel.shape[0]):
+        k = t % per
+        grad_kernel[t] = grad_packed[t // per][:, k * C : (k + 1) * C]
+    grad_offset[...] = grad_rows[0:1, 0:C]
+    grad_stylebias[...] = grad_rows[0:1, C : 2 * C]
+    grad_liftbias[...] = grad_rows[1:2, :]
+    grad_lift[...] = grad_rows[2 : 2 + grad_lift.shape[0], :]
+    grad_style_t[...] = grad_style_in[...]
 
 
 def body(
@@ -381,7 +380,7 @@
     taps = kernel.shape[2] * kernel.shape[3] * kernel.shape[4]
     per = CZ // C
     tiles = (taps + per) // per
-    unit = nz * ny * 8
+    unit = nz * ny * 16
     rows = -(-tiles * C // unit) * unit
     f32, bf16 = jnp.float32, jnp.bfloat16
     dma = pltpu.SemaphoreType.DMA
@@ -389,16 +388,13 @@
     results = pl.pallas_call(
         functools.partial(kernel_body, sizes),
         out_shape=[
-            jax.ShapeDtypeStruct((CX, CY, C, CZ), bf16),
-            jax.ShapeDtypeStruct((taps, C, C), f32),
-            jax.ShapeDtypeStruct((1, C), f32),
-            jax.ShapeDtypeStruct(lift_weight.shape, f32),
-            jax.ShapeDtypeStruct((1, HID), f32),
+            jax.ShapeDtypeStruct(field.shape, bf16),
+            jax.ShapeDtypeStruct((tiles, C, CZ), f32),
+            jax.ShapeDtypeStruct((8, HID), f32),
             jax.ShapeDtypeStruct((C, HID), f32),
-            jax.ShapeDtypeStruct((1, C), f32),
         ],
         in_specs=[vmem] * 9,
-        out_specs=[vmem] * 7,
+        out_specs=[vmem] * 4,
         scratch_shapes=[
             pltpu.VMEM((CX + 2, CY + 2, C, CZ), bf16),
             pltpu.VMEM((CX + 2, CY + 2, C, CZ), bf16),
@@ -409,24 +405,23 @@
             pltpu.VMEM((C, tiles * CZ), bf16),
             pltpu.VMEM((C, tiles * CZ), bf16),
             pltpu.VMEM((tiles, C, CZ), f32),
-            pltpu.VMEM((rows, CZ), f32),
-            pltpu.VMEM((nz - 1, rows // nz, CZ), f32),
-            pltpu.VMEM((rows // nz, CZ), f32),
-            pltpu.VMEM((ny - 1, rows // nz // ny, CZ), f32),
-            pltpu.VMEM((rows // nz // ny, CZ), f32),
-            pltpu.VMEM((nx, rows // nz // ny, CZ), f32),
-            pltpu.VMEM((rows, CZ), f32),
+            pltpu.VMEM((CX, CY, C, CZ), f32),
+            pltpu.VMEM((CY, C, CZ), f32),
+            pltpu.VMEM((rows, CZ), bf16),
+            pltpu.VMEM((nz - 1, rows // nz, CZ), bf16),
+            pltpu.VMEM((rows // nz, CZ), bf16),
+            pltpu.VMEM((nx * ny, rows // nz // ny, CZ), bf16),
+            pltpu.VMEM((rows, CZ), bf16),
             dma((2, 8)), dma((2, 8)), dma((2, 2)), dma((2, 2)),
-            dma((nz - 1,)), dma((nz - 1,)), dma((ny - 1,)), dma((ny - 1,)),
-            dma((nx - 1,)), dma((nx - 1,)), dma((ny - 1,)), dma((ny - 1,)),
-            dma((nz - 1,)), dma((nz - 1,)),
+            dma((nz - 1,)), dma((nz - 1,)), dma((nx * ny - 1,)), dma((nx * ny - 1,)),
+            dma((ny * nz - 1,)), dma((ny * nz - 1,)),
         ],
         compiler_params=pltpu.CompilerParams(
             collective_id=0, has_side_effects=True, vmem_limit_bytes=32 * 1024 * 1024
         ),
     )(
-        jnp.transpose(field, (1, 2, 0, 3)),
-        jnp.transpose(cotangent, (1, 2, 0, 3)),
+        field,
+        cotangent,
         cosmology[None],
         lift_weight,
         lift_bias[None],
@@ -435,9 +430,25 @@
         jnp.transpose(kernel, (2, 3, 4, 0, 1)).reshape(taps, C, C),
         offset[None],
     )
-    grad, grad_kernel, grad_offset, grad_lift, grad_liftbias, grad_style_t, grad_stylebias = results
+    grad, grad_kernel, grad_offset, grad_lift, grad_liftbias, grad_style_t, grad_stylebias = (
+        pl.pallas_call(
+            hand_out,
+            out_shape=[
+                jax.ShapeDtypeStruct(field.shape, bf16),
+                jax.ShapeDtypeStruct((taps, C, C), f32),
+                jax.ShapeDtypeStruct((1, C), f32),
+                jax.ShapeDtypeStruct(lift_weight.shape, f32),
+                jax.ShapeDtypeStruct((1, HID), f32),
+                jax.ShapeDtypeStruct((C, HID), f32),
+                jax.ShapeDtypeStruct((1, C), f32),
+            ],
+            in_specs=[vmem] * 4,
+            out_specs=[vmem] * 7,
+            compiler_params=pltpu.CompilerParams(vmem_limit_bytes=8 * 1024 * 1024),
+        )(*results)
+    )
     return (
-        jnp.transpose(grad, (2, 0, 1, 3)),
+        grad,
         jnp.transpose(grad_kernel.reshape(kernel.shape[2:] + (C, C)), (3, 4, 0, 1, 2)),
         grad_offset[0],
         grad_lift,

time: 42.3 us -> 38.6 us (0.913)
  Pallas kernels: 35.4 us -> 33.3 us
  local copies, waits for them, and re-layouts: 6.08 us -> 4.31 us
    pallas_call x1, Pallas kernels: 35.4 us -> 32.3 us  [body(): pl.pallas_call(functools.partial(kernel_body, sizes), out_shape=[jax.Shap...]
    transpose x1 -> x0, local copies, waits for them, and re-layouts: 1.13 us -> none  [body(): jnp.transpose(cotangent, (1, 2, 0, 3))]
    pallas_call x0 -> x1, Pallas kernels: none -> 0.92 us  [body(): pl.pallas_call(hand_out, out_shape=[jax.ShapeDtypeStruct(field.shape, bf1...]
    unnamed x21 -> x18, local copies, waits for them, and re-layouts: 4.95 us -> 4.31 us
where the time goes in v1:
time: 38.6 us; the launch traced here: 38.3 us
  Pallas kernels  33.3 us (86%)
  local copies, waits for them, and re-layouts  4.31 us (11%)
  between operations  0.69 us (2%)
    pallas_call x1, Pallas kernels, body(): pl.pallas_call(functools.partial(kernel_body, sizes), out_shape=[jax.Shap...  32.3 us
    unnamed x18, local copies, waits for them, and re-layouts  4.31 us
    pallas_call x1, Pallas kernels, body(): pl.pallas_call(hand_out, out_shape=[jax.ShapeDtypeStruct(field.shape, bf1...  0.92 us

profile of v1, /device:TPU:0, one launch (start us, length us, event | category | flops | bytes accessed | tf_op | source)
XLA Modules:
  0.0 38.3 jit_solution(2411012681649117133)
XLA Ops:
  0.6 0.0 copy-start.7
  0.6 0.0 copy-start.8
  0.7 0.0 copy-start.4
  0.7 0.0 copy-start.5
  0.7 0.0 copy-start.6
  0.7 0.6 %copy-done.7 = f32[32]{0:T(128)S(1)} copy-done((f32[32]{0:T(128)S(1)}, f32[32]{0:T(128)}, u32[]{:S(2)}) %copy-start.7) | copy-done | bytes 152
  1.3 0.0 copy-done.8
  1.3 0.0 copy-done.4
  1.4 0.0 copy-done.5
  1.4 0.0 copy-done.6
  1.4 0.0 copy-start
  1.4 1.0 %copy-done = f32[32,32,3,3,3]{1,0,4,3,2:T(8,128)S(1)} copy-done((f32[32,32,3,3,3]{1,0,4,3,2:T(8,128)S(1)}, f32[32,32,3,3,3]{1,0,4,3,2:T(8,128)}, u32[]{:S(2)}) %copy-start) | copy-done | bytes 110616
  2.4 0.0 copy-start.1
  2.4 0.9 %copy-done.1 = bf16[32,3,8,128]{3,2,1,0:T(8,128)(2,1)S(1)} copy-done((bf16[32,3,8,128]{3,2,1,0:T(8,128)(2,1)S(1)}, bf16[32,3,8,128]{3,2,1,0:T(8,128)(2,1)}, u32[]{:S(2)}) %copy-start.1) | copy-done | bytes 196632
  3.3 0.0 copy-start.2
  3.3 0.9 %copy-done.2 = bf16[32,3,8,128]{3,2,1,0:T(8,128)(2,1)S(1)} copy-done((bf16[32,3,8,128]{3,2,1,0:T(8,128)(2,1)S(1)}, bf16[32,3,8,128]{3,2,1,0:T(8,128)(2,1)}, u32[]{:S(2)}) %copy-start.2) | copy-done | bytes 196632
  4.2 0.0 copy-start.3
  4.2 0.8 %copy-done.3 = f32[256,32]{0,1:T(8,128)S(1)} copy-done((f32[256,32]{0,1:T(8,128)S(1)}, f32[256,32]{0,1:T(8,128)}, u32[]{:S(2)}) %copy-start.3) | copy-done | bytes 32792
  5.0 32.3 %shard_map.144 = (bf16[32,3,8,128]{3,2,1,0:T(8,128)(2,1)S(1)}, f32[7,32,128]{2,1,0:T(8,128)S(1)}, f32[8,256]{1,0:T(8,128)S(1)}, f32[32,256]{1,0:T(8,128)S(1)}) custom-call(bf16[32,3,8,128]{3,2,1,0:T(8,128)(2,1)S(1)} %copy-done.1, bf16[32,3,8,128]{3,2,1,0:T(8,128)(2,1)S(1)} %copy-done.2, f32[1,2]{1,0:T(1,128)S(1)} %bitcast.18, f32[2,256]{1,0:T(2,128)S(1)} %copy-done.4, ...), custom_call_target="tpu_custom_call" | custom-call | tf_op jit(solution)/shard_map/pallas_call | solution.py:388
  37.3 0.9 %shard_map.145 = (bf16[32,3,8,128]{3,2,1,0:T(8,128)(2,1)}, f32[27,32,32]{2,1,0:T(8,128)}, f32[1,32]{1,0:T(1,128)}, f32[2,256]{1,0:T(2,128)}, f32[1,256]{1,0:T(1,...) custom-call(bf16[32,3,8,128]{3,2,1,0:T(8,128)(2,1)S(1)} %get-tuple-element.18.grad_in, ...), custom_call_target="tpu_custom_call" | custom-call | tf_op jit(solution)/shard_map/pallas_call | solution.py:434
Async XLA Ops:
  0.6 0.7 %copy-start.7 = (f32[32]{0:T(128)S(1)}, f32[32]{0:T(128)}, u32[]{:S(2)}) copy-start(f32[32]{0:T(128)} %param.15) | copy-start | bytes 388
  0.6 0.7 %copy-start.8 = (f32[32]{0:T(128)S(1)}, f32[32]{0:T(128)}, u32[]{:S(2)}) copy-start(f32[32]{0:T(128)} %param.17) | copy-start | bytes 388
  0.7 0.7 %copy-start.4 = (f32[2,256]{1,0:T(2,128)S(1)}, f32[2,256]{1,0:T(2,128)}, u32[]{:S(2)}) copy-start(f32[2,256]{1,0:T(2,128)} %lift_weight.1) | copy-start | bytes 6148
  0.7 0.7 %copy-start.5 = (f32[256]{0:T(256)S(1)}, f32[256]{0:T(256)}, u32[]{:S(2)}) copy-start(f32[256]{0:T(256)} %param.13) | copy-start | bytes 3076
  0.7 0.7 %copy-start.6 = (f32[2]{0:T(128)S(1)}, f32[2]{0:T(128)}, u32[]{:S(2)}) copy-start(f32[2]{0:T(128)} %param.11) | copy-start | bytes 28
  1.4 1.0 %copy-start = (f32[32,32,3,3,3]{1,0,4,3,2:T(8,128)S(1)}, f32[32,32,3,3,3]{1,0,4,3,2:T(8,128)}, u32[]{:S(2)}) copy-start(f32[32,32,3,3,3]{1,0,4,3,2:T(8,128)} %param.16) | copy-start | bytes 331780
  2.4 0.9 %copy-start.1 = (bf16[32,3,8,128]{3,2,1,0:T(8,128)(2,1)S(1)}, bf16[32,3,8,128]{3,2,1,0:T(8,128)(2,1)}, u32[]{:S(2)}) copy-start(bf16[32,3,8,128]{3,2,1,0:T(8,128)(2,1)} %field.1) | copy-start | bytes 589828
  3.3 0.9 %copy-start.2 = (bf16[32,3,8,128]{3,2,1,0:T(8,128)(2,1)S(1)}, bf16[32,3,8,128]{3,2,1,0:T(8,128)(2,1)}, u32[]{:S(2)}) copy-start(bf16[32,3,8,128]{3,2,1,0:T(8,128)(2,1)} %cotangent.1) | copy-start | bytes 589828
  4.2 0.8 %copy-start.3 = (f32[256,32]{0,1:T(8,128)S(1)}, f32[256,32]{0,1:T(8,128)}, u32[]{:S(2)}) copy-start(f32[256,32]{0,1:T(8,128)} %param.14) | copy-start | bytes 98308

commit v2 on v1

--- a/solution.py
+++ b/solution.py
@@ -20,9 +20,11 @@
 
 def kernel_body(
     sizes,
+    field_hbm, cotangent_hbm, cosmology_hbm, lift_weight_hbm, lift_bias_hbm, style_hbm,
+    style_bias_hbm, kernel_hbm, offset_hbm,
+    grad, grad_packed, grad_rows, grad_style_t,
     field, cotangent, cosmology, lift_weight, lift_bias, style_t, style_bias, kernel, offset,
-    grad, grad_packed, grad_rows, grad_style_t,
-    field_ext, up_ext, field_taps, up_taps, edge_out, edge_in, w_fwd, w_bwd, packed, cot, turned_back,
+    fetch_sem, field_ext, up_ext, field_taps, up_taps, edge_out, edge_in, w_fwd, w_bwd, packed, cot, turned_back,
     share, from_z, part_z, from_xy, total,
     xy_send, xy_recv, z_send, z_recv, rz_send, rz_recv, rxy_send, rxy_recv, g_send, g_recv,
 ):
@@ -32,6 +34,19 @@
     taps = kernel.shape[0]
     per = CZ // C
     tiles = (taps + per) // per
+    fetches = [
+        pltpu.make_async_copy(source, held, fetch_sem.at[k])
+        for k, (source, held) in enumerate(
+            zip(
+                (field_hbm, kernel_hbm, cosmology_hbm, lift_weight_hbm, lift_bias_hbm, style_hbm,
+                 style_bias_hbm, offset_hbm, cotangent_hbm),
+                (field, kernel, cosmology, lift_weight, lift_bias, style_t, style_bias, offset,
+                 cotangent),
+            )
+        )
+    ]
+    for fetch in fetches:
+        fetch.start()
     me_x, me_y, me_z = (lax.axis_index("gx"), lax.axis_index("gy"), lax.axis_index("gz"))
 
     def at(dx=0, dy=0, dz=0):
@@ -41,11 +56,18 @@
             lax.rem(me_z + (dz + nz), nz) if dz else me_z,
         )
 
-    partners = [at(dx, dy) for dx, dy in SIDES]
     plane_xy = [(dx, dy) for dx in range(nx) for dy in range(ny) if (dx, dy) != (0, 0)]
     plane_yz = [(dy, dz) for dy in range(ny) for dz in range(nz) if (dy, dz) != (0, 0)]
-    partners += [at(dx, dy) for dx, dy in plane_xy]
-    partners += [at(0, dy, dz) for dy, dz in plane_yz]
+    edge_dx = (0, 1) if nx == 2 else (-1, 0, 1)
+    corners = [(dx, dy, dz) for dz in (1, -1) for dx in edge_dx for dy in (-1, 0, 1)]
+    steps = {}
+    for dx, dy, dz in (
+        [(dx, dy, 0) for dx, dy in SIDES + tuple(plane_xy)]
+        + [(0, dy, dz) for dy, dz in plane_yz]
+        + corners
+    ):
+        steps[(dx % nx, dy % ny, dz % nz)] = True
+    partners = [at(*step) for step in steps]
     barrier = pltpu.get_barrier_semaphore()
     for partner in partners:
         pl.semaphore_signal(barrier, inc=1, device_id=partner, device_id_type=MESH)
@@ -79,30 +101,36 @@
 
     def edge_copies(which):
         return [
-            remote(edge_out.at[which], edge_in.at[which, 0], z_send.at[which, 0],
-                   z_recv.at[which, 0], at(dz=1)),
-            remote(edge_out.at[which], edge_in.at[which, 1], z_send.at[which, 1],
-                   z_recv.at[which, 1], at(dz=-1)),
+            remote(edge_out.at[which],
+                   edge_in.at[which, 0 if dz > 0 else 1, 1 - dx, 1 - dy],
+                   z_send.at[which, k], z_recv.at[which, k], at(dx, dy, dz))
+            for k, (dx, dy, dz) in enumerate(corners)
         ]
 
     def pack_edges(which, ext):
-        def plane(p, edges):
+        edges = jnp.zeros((C, CZ), jnp.float32)
+        for x in range(CX):
+            for y in range(CY):
+                row = x * CY + y
+                rolled = pltpu.roll(ext[x + 1, y + 1].astype(jnp.float32), 1 + 2 * row, 1)
+                edges = jnp.where(group == row, rolled, edges)
+        edge_out[which] = edges.astype(jnp.bfloat16)
+
+    def build_taps(which, ext, out):
+        def plane(p, carry):
+            first, final = p == 0, p == CX + 1
+            place_x = jnp.where(first, 0, jnp.where(final, 0 if nx == 2 else 2, 1))
+            x = jnp.where(first, CX - 1, jnp.where(final, 0, p - 1))
+            tiles_at = {}
             for y in range(EY):
-                row = p * EY + y
-                rolled = pltpu.roll(ext[p, y].astype(jnp.float32), 1 + 2 * row, 1)
-                edges = jnp.where(group == row, rolled, edges)
-            return edges
-
-        edges = lax.fori_loop(0, CX + 2, plane, jnp.zeros((C, CZ), jnp.float32))
-        edge_out[which] = edges.astype(jnp.bfloat16)
-
-    def build_taps(which, ext, out):
-        before = edge_in[which, 0].astype(jnp.float32)
-        after = edge_in[which, 1].astype(jnp.float32)
-
-        def plane(p, carry):
-            for y in range(EY):
-                row = p * EY + y
+                place_y, line = (0, CY - 1) if y == 0 else (2, 0) if y == EY - 1 else (1, y - 1)
+                if place_y not in tiles_at:
+                    tiles_at[place_y] = [
+                        edge_in[which, side, place_x, place_y].astype(jnp.float32)
+                        for side in (0, 1)
+                    ]
+                before, after = tiles_at[place_y]
+                row = x * CY + line
                 mid = ext[p, y]
                 wide = mid.astype(jnp.float32)
                 low = jnp.where(lanes == 0, pltpu.roll(before, lax.rem(CZ - 2 * row, CZ), 1),
@@ -116,20 +144,33 @@
 
         lax.fori_loop(0, CX + 2, plane, 0)
 
-    def columns(source, x, y):
-        both = []
-        for k in range(2):
-            planes = [source[x + a, pl.ds(y + k, 3)].reshape(9 * C, CZ) for a in range(3)]
-            both.append(jnp.concatenate(planes, axis=0))
-        return jnp.concatenate(both, axis=1)
-
+    def columns(source, p, y):
+        return jnp.concatenate(
+            [source[p, pl.ds(y + k, 3)].reshape(9 * C, CZ) for k in range(2)], axis=1
+        )
+
+    def convolve(weights, source, y):
+        results = [None] * CX
+        for p in range(CX + 2):
+            product = jnp.dot(weights[...], columns(source, p, y),
+                              preferred_element_type=jnp.float32)
+            for a in range(3):
+                if 0 <= p - a < CX:
+                    term = product[a * C : (a + 1) * C]
+                    results[p - a] = term if results[p - a] is None else results[p - a] + term
+        return results
+
+    fetches[0].wait()
     for x in range(CX):
         turned_x = jnp.swapaxes(field[:, x].astype(jnp.float32), 0, 1)
         field_ext[x + 1, 1 : CY + 1] = turned_x.astype(jnp.bfloat16)
+    pack_edges(0, field_ext)
     pl.semaphore_wait(barrier, len(partners))
-    field_sides = side_copies(0, field_ext, 1, field_ext)
+    field_sides = side_copies(0, field_ext, 1, field_ext) + edge_copies(0)
     for copy in field_sides:
         copy.start()
+    for fetch in fetches[1:]:
+        fetch.wait()
 
     eye = lax.broadcasted_iota(jnp.int32, (C, C), 0) == lax.broadcasted_iota(jnp.int32, (C, C), 1)
 
@@ -161,14 +202,16 @@
     inv_norm = lax.rsqrt(jnp.sum(squares, axis=1, keepdims=True) + demod_eps)
     turned = []
     for j in range(tiles):
-        scaled = packed[j] * styles_wide * inv_norm
-        w_fwd[:, j * CZ : (j + 1) * CZ] = scaled.astype(jnp.bfloat16)
-        flat = scaled.T
+        flat = (packed[j] * styles_wide * inv_norm).T
         turned += [flat[k * C : (k + 1) * C] for k in range(per)]
-    turned = turned[:taps][::-1] + [jnp.zeros((C, C), jnp.float32)] * (tiles * per - taps)
-    for j in range(tiles):
-        w_bwd[:, j * CZ : (j + 1) * CZ] = jnp.concatenate(
-            turned[per * j : per * (j + 1)], axis=1
+    turned = turned[:taps][::-1]
+    for a in range(3):
+        taken = range(9 * a, 9 * a + 9)
+        w_fwd[a * C : (a + 1) * C, :] = jnp.concatenate(
+            [kernel[t] * styles * inv_norm for t in taken], axis=1
+        ).astype(jnp.bfloat16)
+        w_bwd[a * C : (a + 1) * C, :] = jnp.concatenate(
+            [turned[t] for t in taken], axis=1
         ).astype(jnp.bfloat16)
     offset_column = to_column(offset[...])
     for x in range(CX):
@@ -176,47 +219,50 @@
 
     for copy in field_sides:
         copy.wait()
-    pack_edges(0, field_ext)
-    field_edges = edge_copies(0)
-    for copy in field_edges:
-        copy.start()
-    for copy in field_edges:
-        copy.wait()
     build_taps(0, field_ext, field_taps)
 
     depth = taps * C
 
-    def forward(x, carry):
-        for y in range(0, CY, 2):
-            preact = jnp.dot(w_fwd[:, :depth], columns(field_taps, x, y),
-                             preferred_element_type=jnp.float32) + offset_column
+    def forward(at_pair, carry):
+        y = 2 * at_pair
+        for x, sums in enumerate(convolve(w_fwd, field_taps, y)):
             above = jnp.concatenate([cot[x, y], cot[x, y + 1]], axis=1)
-            upstream = (above * silu_slope(preact)).astype(jnp.bfloat16)
+            upstream = (above * silu_slope(sums + offset_column)).astype(jnp.bfloat16)
             up_ext[x + 1, y + 1] = upstream[:, :CZ]
             up_ext[x + 1, y + 2] = upstream[:, CZ:]
         return carry
 
-    lax.fori_loop(0, CX, forward, 0)
-    up_sides = side_copies(1, up_ext, 1, up_ext)
+    lax.fori_loop(0, CY // 2, forward, 0)
+    pack_edges(1, up_ext)
+    up_sides = side_copies(1, up_ext, 1, up_ext) + edge_copies(1)
     for copy in up_sides:
         copy.start()
 
-    def weigh(x, carry):
-        sums, offsets = carry
-        for y in range(0, CY, 2):
+    def weigh(at_pair, carry):
+        y = 2 * at_pair
+        sums, offsets = list(carry[:3]), carry[3]
+        ups = []
+        for x in range(CX):
             upstream = jnp.concatenate([up_ext[x + 1, y + 1], up_ext[x + 1, y + 2]], axis=1)
-            sums = sums + lax.dot_general(
-                upstream, columns(field_taps, x, y), (((1,), (1,)), ((), ())),
+            wide = upstream.astype(jnp.float32)
+            offsets = offsets + wide[:, :CZ] + wide[:, CZ:]
+            ups.append(upstream)
+        for p in range(CX + 2):
+            taken = [a for a in range(3) if 0 <= p - a < CX]
+            product = lax.dot_general(
+                jnp.concatenate([ups[p - a] for a in taken], axis=0),
+                columns(field_taps, p, y), (((1,), (1,)), ((), ())),
                 preferred_element_type=jnp.float32,
             )
-            wide = upstream.astype(jnp.float32)
-            offsets = offsets + wide[:, :CZ] + wide[:, CZ:]
-        return (sums, offsets)
-
-    sums, offsets = lax.fori_loop(
-        0, CX, weigh,
-        (jnp.zeros((C, depth), jnp.float32), jnp.zeros((C, CZ), jnp.float32)),
+            for k, a in enumerate(taken):
+                sums[a] = sums[a] + product[k * C : (k + 1) * C]
+        return (*sums, offsets)
+
+    *sums, offsets = lax.fori_loop(
+        0, CY // 2, weigh,
+        (jnp.zeros((C, 9 * C), jnp.float32),) * 3 + (jnp.zeros((C, CZ), jnp.float32),),
     )
+    sums = jnp.concatenate(sums, axis=1)
     offset_sum = jnp.sum(offsets, axis=1, keepdims=True)
     for j in range(share.shape[0] // C):
         if (j + 1) * CZ <= depth:
@@ -242,13 +288,6 @@
         reduce_z.append(remote(share.at[rows_at(there[2] * rows_z, rows_z)], from_z.at[k - 1],
                                rz_send.at[k - 1], rz_recv.at[k - 1], there))
     for copy in reduce_z:
-        copy.start()
-
-    for copy in up_sides:
-        copy.wait()
-    pack_edges(1, up_ext)
-    up_edges = edge_copies(1)
-    for copy in up_edges:
         copy.start()
 
     for copy in reduce_z:
@@ -267,20 +306,19 @@
         copy.start()
     from_xy[my_slot] = part_z[rows_at(me_y * rows_y, rows_y), :]
 
-    for copy in up_edges:
+    for copy in up_sides:
         copy.wait()
     build_taps(1, up_ext, up_taps)
 
-    def backward(x, carry):
-        for y in range(0, CY, 2):
-            result = jnp.dot(w_bwd[:, :depth], columns(up_taps, x, y),
-                             preferred_element_type=jnp.float32)
-            turned_back[y] = result[:, :CZ]
-            turned_back[y + 1] = result[:, CZ:]
-        grad[:, x] = jnp.swapaxes(turned_back[...], 0, 1).astype(jnp.bfloat16)
+    def backward(at_pair, carry):
+        y = 2 * at_pair
+        for x, result in enumerate(convolve(w_bwd, up_taps, y)):
+            turned_back[x, y] = result[:, :CZ]
+            turned_back[x, y + 1] = result[:, CZ:]
         return carry
 
-    lax.fori_loop(0, 1, backward, 0)
+    middle = CY // 4
+    lax.fori_loop(0, middle, backward, 0)
 
     for copy in reduce_xy:
         copy.wait()
@@ -295,7 +333,9 @@
     ]
     for copy in gather:
         copy.start()
-    lax.fori_loop(1, CX, backward, 0)
+    lax.fori_loop(middle, CY // 2, backward, 0)
+    for x in range(CX):
+        grad[:, x] = jnp.swapaxes(turned_back[x], 0, 1).astype(jnp.bfloat16)
     for copy in gather:
         copy.wait()
 
@@ -393,31 +433,41 @@
             jax.ShapeDtypeStruct((8, HID), f32),
             jax.ShapeDtypeStruct((C, HID), f32),
         ],
-        in_specs=[vmem] * 9,
+        in_specs=[pl.BlockSpec(memory_space=pltpu.HBM)] * 9,
         out_specs=[vmem] * 4,
         scratch_shapes=[
+            pltpu.VMEM(field.shape, bf16),
+            pltpu.VMEM(field.shape, bf16),
+            pltpu.VMEM((1, cosmology.shape[0]), f32),
+            pltpu.VMEM(lift_weight.shape, f32),
+            pltpu.VMEM((1, HID), f32),
+            pltpu.VMEM((C, HID), f32),
+            pltpu.VMEM((1, C), f32),
+            pltpu.VMEM((taps, C, C), f32),
+            pltpu.VMEM((1, C), f32),
+            dma((9,)),
             pltpu.VMEM((CX + 2, CY + 2, C, CZ), bf16),
             pltpu.VMEM((CX + 2, CY + 2, C, CZ), bf16),
             pltpu.VMEM((CX + 2, CY + 2, 3 * C, CZ), bf16),
             pltpu.VMEM((CX + 2, CY + 2, 3 * C, CZ), bf16),
             pltpu.VMEM((2, C, CZ), bf16),
-            pltpu.VMEM((2, 2, C, CZ), bf16),
-            pltpu.VMEM((C, tiles * CZ), bf16),
-            pltpu.VMEM((C, tiles * CZ), bf16),
+            pltpu.VMEM((2, 2, 3, 3, C, CZ), bf16),
+            pltpu.VMEM((3 * C, 9 * C), bf16),
+            pltpu.VMEM((3 * C, 9 * C), bf16),
             pltpu.VMEM((tiles, C, CZ), f32),
             pltpu.VMEM((CX, CY, C, CZ), f32),
-            pltpu.VMEM((CY, C, CZ), f32),
+            pltpu.VMEM((CX, CY, C, CZ), f32),
             pltpu.VMEM((rows, CZ), bf16),
             pltpu.VMEM((nz - 1, rows // nz, CZ), bf16),
             pltpu.VMEM((rows // nz, CZ), bf16),
             pltpu.VMEM((nx * ny, rows // nz // ny, CZ), bf16),
             pltpu.VMEM((rows, CZ), bf16),
-            dma((2, 8)), dma((2, 8)), dma((2, 2)), dma((2, 2)),
+            dma((2, 8)), dma((2, 8)), dma((2, 18)), dma((2, 18)),
             dma((nz - 1,)), dma((nz - 1,)), dma((nx * ny - 1,)), dma((nx * ny - 1,)),
             dma((ny * nz - 1,)), dma((ny * nz - 1,)),
         ],
         compiler_params=pltpu.CompilerParams(
-            collective_id=0, has_side_effects=True, vmem_limit_bytes=32 * 1024 * 1024
+            collective_id=0, has_side_effects=True, vmem_limit_bytes=60 * 1024 * 1024
         ),
     )(
         field,
@@ -444,7 +494,7 @@
             ],
             in_specs=[vmem] * 4,
             out_specs=[vmem] * 7,
-            compiler_params=pltpu.CompilerParams(vmem_limit_bytes=8 * 1024 * 1024),
+            compiler_params=pltpu.CompilerParams(vmem_limit_bytes=60 * 1024 * 1024),
         )(*results)
     )
     return (

time: 38.6 us -> 33.4 us (0.87)
  local copies, waits for them, and re-layouts: 4.31 us -> 0 us
  Pallas kernels: 33.3 us -> 32.6 us
    unnamed x18 -> x0, local copies, waits for them, and re-layouts: 4.31 us -> none
    pallas_call x1, Pallas kernels: 32.3 us -> 30.7 us  [body(): pl.pallas_call(functools.partial(kernel_body, sizes), out_shape=[jax.Shap...]
    pallas_call x1, Pallas kernels: 0.92 us -> 1.91 us  [body(): pl.pallas_call(hand_out, out_shape=[jax.ShapeDtypeStruct(field.shape, bf1...]
where the time goes in v2:
time: 33.4 us; the launch traced here: 33.2 us
  Pallas kernels  32.6 us (98%)
  between operations  0.64 us (2%)
    pallas_call x1, Pallas kernels, body(): pl.pallas_call(functools.partial(kernel_body, sizes), out_shape=[jax.Shap...  30.7 us
    pallas_call x1, Pallas kernels, body(): pl.pallas_call(hand_out, out_shape=[jax.ShapeDtypeStruct(field.shape, bf1...  1.91 us

profile of v2, /device:TPU:0, one launch (start us, length us, event | category | flops | bytes accessed | tf_op | source)
XLA Modules:
  0.0 33.2 jit_solution(8610548208506037403)
XLA Ops:
  0.6 30.7 %shard_map.144 = (bf16[32,3,8,128]{3,2,1,0:T(8,128)(2,1)}, f32[7,32,128]{2,1,0:T(8,128)}, f32[8,256]{1,0:T(8,128)}, f32[32,256]{1,0:T(8,128)}) custom-call(bf16[32,3,8,128]{3,2,1,0:T(8,128)(2,1)} %field_hbm.1, bf16[32,3,8,128]{3,2,1,0:T(8,128)(2,1)} %cotangent_hbm.1, f32[1,2]{1,0:T(1,128)} %bitcast.18, f32[2,256]{1,0:T(2,128)} %lift_weight_hbm.1, ...), custom_call_target="tpu_custom_call" | custom-call | tf_op jit(solution)/shard_map/pallas_call | solution.py:428
  31.3 1.9 %shard_map.145 = (bf16[32,3,8,128]{3,2,1,0:T(8,128)(2,1)}, f32[27,32,32]{2,1,0:T(8,128)}, f32[1,32]{1,0:T(1,128)}, f32[2,256]{1,0:T(2,128)}, f32[1,256]{1,0:T(1,...) custom-call(bf16[32,3,8,128]{3,2,1,0:T(8,128)(2,1)} %get-tuple-element.18.grad_in, ...), custom_call_target="tpu_custom_call" | custom-call | tf_op jit(solution)/shard_map/pallas_call | solution.py:484

commit v3 on v2

--- a/solution.py
+++ b/solution.py
@@ -24,7 +24,7 @@
     style_bias_hbm, kernel_hbm, offset_hbm,
     grad, grad_packed, grad_rows, grad_style_t,
     field, cotangent, cosmology, lift_weight, lift_bias, style_t, style_bias, kernel, offset,
-    fetch_sem, field_ext, up_ext, field_taps, up_taps, edge_out, edge_in, w_fwd, w_bwd, packed, cot, turned_back,
+    fetch_sem, field_ext, up_ext, field_taps, up_taps, edge_out, edge_in, w_fwd, w_bwd, packed, cot, turned_back, held,
     share, from_z, part_z, from_xy, total,
     xy_send, xy_recv, z_send, z_recv, rz_send, rz_recv, rxy_send, rxy_recv, g_send, g_recv,
 ):
@@ -35,8 +35,8 @@
     per = CZ // C
     tiles = (taps + per) // per
     fetches = [
-        pltpu.make_async_copy(source, held, fetch_sem.at[k])
-        for k, (source, held) in enumerate(
+        pltpu.make_async_copy(source, there, fetch_sem.at[k])
+        for k, (source, there) in enumerate(
             zip(
                 (field_hbm, kernel_hbm, cosmology_hbm, lift_weight_hbm, lift_bias_hbm, style_hbm,
                  style_bias_hbm, offset_hbm, cotangent_hbm),
@@ -85,27 +85,36 @@
             return pl.ds(first + count - 1, 1), pl.ds(0, 1)
         return pl.ds(first, 1), pl.ds(count + 1, 1)
 
-    def side_copies(which, source, first, ext):
+    def side_copies(which, ext, near):
         copies = []
         for at_side, (dx, dy) in enumerate(SIDES):
-            sx, tx = span(dx, CX, first)
-            sy, ty = span(dy, CY, first)
-            copies.append(
-                remote(source.at[sx, sy], ext.at[tx, ty], xy_send.at[which, at_side],
-                       xy_recv.at[which, at_side], at(dx, dy))
-            )
+            if (dx == 0) == near:
+                sx, tx = span(dx, CX, 1)
+                sy, ty = span(dy, CY, 1)
+                copies.append(
+                    remote(ext.at[sx, sy], ext.at[tx, ty], xy_send.at[which, at_side],
+                           xy_recv.at[which, at_side], at(dx, dy))
+                )
         return copies
 
     lanes = lax.broadcasted_iota(jnp.int32, (C, CZ), 1)
     group = lax.div(lanes, 2)
 
-    def edge_copies(which):
+    def edge_copies(which, near):
         return [
             remote(edge_out.at[which],
                    edge_in.at[which, 0 if dz > 0 else 1, 1 - dx, 1 - dy],
                    z_send.at[which, k], z_recv.at[which, k], at(dx, dy, dz))
             for k, (dx, dy, dz) in enumerate(corners)
+            if (dx == 0) == near
         ]
+
+    def exchange(which, ext):
+        near = side_copies(which, ext, True) + edge_copies(which, True)
+        far = side_copies(which, ext, False) + edge_copies(which, False)
+        for copy in near + far:
+            copy.start()
+        return near, far
 
     def pack_edges(which, ext):
         edges = jnp.zeros((C, CZ), jnp.float32)
@@ -116,48 +125,53 @@
                 edges = jnp.where(group == row, rolled, edges)
         edge_out[which] = edges.astype(jnp.bfloat16)
 
-    def build_taps(which, ext, out):
-        def plane(p, carry):
-            first, final = p == 0, p == CX + 1
-            place_x = jnp.where(first, 0, jnp.where(final, 0 if nx == 2 else 2, 1))
-            x = jnp.where(first, CX - 1, jnp.where(final, 0, p - 1))
-            tiles_at = {}
-            for y in range(EY):
-                place_y, line = (0, CY - 1) if y == 0 else (2, 0) if y == EY - 1 else (1, y - 1)
-                if place_y not in tiles_at:
-                    tiles_at[place_y] = [
-                        edge_in[which, side, place_x, place_y].astype(jnp.float32)
-                        for side in (0, 1)
-                    ]
-                before, after = tiles_at[place_y]
-                row = x * CY + line
-                mid = ext[p, y]
-                wide = mid.astype(jnp.float32)
-                low = jnp.where(lanes == 0, pltpu.roll(before, lax.rem(CZ - 2 * row, CZ), 1),
-                                pltpu.roll(wide, 1, 1))
-                high = jnp.where(lanes == CZ - 1, pltpu.roll(after, CZ - 2 - 2 * row, 1),
-                                 pltpu.roll(wide, CZ - 1, 1))
-                out[p, y, 0:C] = low.astype(jnp.bfloat16)
-                out[p, y, C : 2 * C] = mid
-                out[p, y, 2 * C : 3 * C] = high.astype(jnp.bfloat16)
+    def build_taps(which, ext, out, p, place_x, x):
+        tiles_at = {}
+        for y in range(EY):
+            place_y, line = (0, CY - 1) if y == 0 else (2, 0) if y == EY - 1 else (1, y - 1)
+            if place_y not in tiles_at:
+                tiles_at[place_y] = [
+                    edge_in[which, side, place_x, place_y].astype(jnp.float32)
+                    for side in (0, 1)
+                ]
+            before, after = tiles_at[place_y]
+            row = x * CY + line
+            mid = ext[p, y]
+            wide = mid.astype(jnp.float32)
+            low = jnp.where(lanes == 0, pltpu.roll(before, lax.rem(CZ - 2 * row, CZ), 1),
+                            pltpu.roll(wide, 1, 1))
+            high = jnp.where(lanes == CZ - 1, pltpu.roll(after, CZ - 2 - 2 * row, 1),
+                             pltpu.roll(wide, CZ - 1, 1))
+            out[p, y, 0:C] = low.astype(jnp.bfloat16)
+            out[p, y, C : 2 * C] = mid
+            out[p, y, 2 * C : 3 * C] = high.astype(jnp.bfloat16)
+
+    def build_near(which, ext, out):
+        def plane(x, carry):
+            build_taps(which, ext, out, x + 1, 1, x)
             return carry
 
-        lax.fori_loop(0, CX + 2, plane, 0)
+        lax.fori_loop(0, CX, plane, 0)
+
+    def build_far(which, ext, out):
+        build_taps(which, ext, out, 0, 0, CX - 1)
+        build_taps(which, ext, out, CX + 1, 0 if nx == 2 else 2, 0)
 
     def columns(source, p, y):
         return jnp.concatenate(
             [source[p, pl.ds(y + k, 3)].reshape(9 * C, CZ) for k in range(2)], axis=1
         )
 
-    def convolve(weights, source, y):
-        results = [None] * CX
-        for p in range(CX + 2):
-            product = jnp.dot(weights[...], columns(source, p, y),
-                              preferred_element_type=jnp.float32)
-            for a in range(3):
-                if 0 <= p - a < CX:
-                    term = product[a * C : (a + 1) * C]
-                    results[p - a] = term if results[p - a] is None else results[p - a] + term
+    near_planes, far_planes = range(1, CX + 1), (0, CX + 1)
+
+    def convolve(weights, source, y, planes, results):
+        for p in planes:
+            taken = [a for a in range(3) if 0 <= p - a < CX]
+            product = jnp.dot(weights[taken[0] * C : (taken[-1] + 1) * C, :],
+                              columns(source, p, y), preferred_element_type=jnp.float32)
+            for k, a in enumerate(taken):
+                term = product[k * C : (k + 1) * C]
+                results[p - a] = term if results[p - a] is None else results[p - a] + term
         return results
 
     fetches[0].wait()
@@ -166,9 +180,7 @@
         field_ext[x + 1, 1 : CY + 1] = turned_x.astype(jnp.bfloat16)
     pack_edges(0, field_ext)
     pl.semaphore_wait(barrier, len(partners))
-    field_sides = side_copies(0, field_ext, 1, field_ext) + edge_copies(0)
-    for copy in field_sides:
-        copy.start()
+    field_near, field_far = exchange(0, field_ext)
     for fetch in fetches[1:]:
         fetch.wait()
 
@@ -217,26 +229,45 @@
     for x in range(CX):
         cot[x] = jnp.swapaxes(cotangent[:, x].astype(jnp.float32), 0, 1)
 
-    for copy in field_sides:
-        copy.wait()
-    build_taps(0, field_ext, field_taps)
+    for copy in field_near:
+        copy.wait()
+    build_near(0, field_ext, field_taps)
 
     depth = taps * C
 
-    def forward(at_pair, carry):
+    edge_x = sorted({0, CX - 1})
+
+    def finish(x, y, sums):
+        above = jnp.concatenate([cot[x, y], cot[x, y + 1]], axis=1)
+        upstream = (above * silu_slope(sums + offset_column)).astype(jnp.bfloat16)
+        up_ext[x + 1, y + 1] = upstream[:, :CZ]
+        up_ext[x + 1, y + 2] = upstream[:, CZ:]
+
+    def forward_near(at_pair, carry):
         y = 2 * at_pair
-        for x, sums in enumerate(convolve(w_fwd, field_taps, y)):
-            above = jnp.concatenate([cot[x, y], cot[x, y + 1]], axis=1)
-            upstream = (above * silu_slope(sums + offset_column)).astype(jnp.bfloat16)
-            up_ext[x + 1, y + 1] = upstream[:, :CZ]
-            up_ext[x + 1, y + 2] = upstream[:, CZ:]
+        results = convolve(w_fwd, field_taps, y, near_planes, [None] * CX)
+        for x, sums in enumerate(results):
+            if x in edge_x:
+                held[x, at_pair] = sums
+            else:
+                finish(x, y, sums)
         return carry
 
-    lax.fori_loop(0, CY // 2, forward, 0)
+    def forward_far(at_pair, carry):
+        y = 2 * at_pair
+        results = [held[x, at_pair] if x in edge_x else None for x in range(CX)]
+        results = convolve(w_fwd, field_taps, y, far_planes, results)
+        for x in edge_x:
+            finish(x, y, results[x])
+        return carry
+
+    lax.fori_loop(0, CY // 2, forward_near, 0)
+    for copy in field_far:
+        copy.wait()
+    build_far(0, field_ext, field_taps)
+    lax.fori_loop(0, CY // 2, forward_far, 0)
     pack_edges(1, up_ext)
-    up_sides = side_copies(1, up_ext, 1, up_ext) + edge_copies(1)
-    for copy in up_sides:
-        copy.start()
+    up_near, up_far = exchange(1, up_ext)
 
     def weigh(at_pair, carry):
         y = 2 * at_pair
@@ -290,6 +321,10 @@
     for copy in reduce_z:
         copy.start()
 
+    for copy in up_near:
+        copy.wait()
+    build_near(1, up_ext, up_taps)
+
     for copy in reduce_z:
         copy.wait()
     mine = share[rows_at(me_z * rows_z, rows_z), :].astype(jnp.float32)
@@ -306,19 +341,21 @@
         copy.start()
     from_xy[my_slot] = part_z[rows_at(me_y * rows_y, rows_y), :]
 
-    for copy in up_sides:
-        copy.wait()
-    build_taps(1, up_ext, up_taps)
-
-    def backward(at_pair, carry):
+    def backward_near(at_pair, carry):
         y = 2 * at_pair
-        for x, result in enumerate(convolve(w_bwd, up_taps, y)):
-            turned_back[x, y] = result[:, :CZ]
-            turned_back[x, y + 1] = result[:, CZ:]
+        for x, sums in enumerate(convolve(w_bwd, up_taps, y, near_planes, [None] * CX)):
+            held[x, at_pair] = sums
         return carry
 
-    middle = CY // 4
-    lax.fori_loop(0, middle, backward, 0)
+    def backward_far(at_pair, carry):
+        y = 2 * at_pair
+        results = [held[x, at_pair] for x in range(CX)]
+        for x, sums in enumerate(convolve(w_bwd, up_taps, y, far_planes, results)):
+            turned_back[x, y] = sums[:, :CZ]
+            turned_back[x, y + 1] = sums[:, CZ:]
+        return carry
+
+    lax.fori_loop(0, CY // 2, backward_near, 0)
 
     for copy in reduce_xy:
         copy.wait()
@@ -333,7 +370,10 @@
     ]
     for copy in gather:
         copy.start()
-    lax.fori_loop(middle, CY // 2, backward, 0)
+    for copy in up_far:
+        copy.wait()
+    build_far(1, up_ext, up_taps)
+    lax.fori_loop(0, CY // 2, backward_far, 0)
     for x in range(CX):
         grad[:, x] = jnp.swapaxes(turned_back[x], 0, 1).astype(jnp.bfloat16)
     for copy in gather:
@@ -457,6 +497,7 @@
             pltpu.VMEM((tiles, C, CZ), f32),
             pltpu.VMEM((CX, CY, C, CZ), f32),
             pltpu.VMEM((CX, CY, C, CZ), f32),
+            pltpu.VMEM((CX, CY // 2, C, 2 * CZ), f32),
             pltpu.VMEM((rows, CZ), bf16),
             pltpu.VMEM((nz - 1, rows // nz, CZ), bf16),
             pltpu.VMEM((rows // nz, CZ), bf16),

time: 33.4 us -> 33.3 us (level)
  no operation moved by 1% of the time
where the time goes in v3:
time: 33.3 us; the launch traced here: 33.2 us
  Pallas kernels  32.5 us (98%)
  between operations  0.64 us (2%)
    pallas_call x1, Pallas kernels, body(): pl.pallas_call(functools.partial(kernel_body, sizes), out_shape=[jax.Shap...  30.6 us
    pallas_call x1, Pallas kernels, body(): pl.pallas_call(hand_out, out_shape=[jax.ShapeDtypeStruct(field.shape, bf1...  1.91 us

profile of v3, /device:TPU:0, one launch (start us, length us, event | category | flops | bytes accessed | tf_op | source)
XLA Modules:
  0.0 33.2 jit_solution(12722197851342757073)
XLA Ops:
  0.6 30.6 %shard_map.144 = (bf16[32,3,8,128]{3,2,1,0:T(8,128)(2,1)}, f32[7,32,128]{2,1,0:T(8,128)}, f32[8,256]{1,0:T(8,128)}, f32[32,256]{1,0:T(8,128)}) custom-call(bf16[32,3,8,128]{3,2,1,0:T(8,128)(2,1)} %field_hbm.1, bf16[32,3,8,128]{3,2,1,0:T(8,128)(2,1)} %cotangent_hbm.1, f32[1,2]{1,0:T(1,128)} %bitcast.18, f32[2,256]{1,0:T(2,128)} %lift_weight_hbm.1, ...), custom_call_target="tpu_custom_call" | custom-call | tf_op jit(solution)/shard_map/pallas_call | solution.py:468
  31.3 1.9 %shard_map.145 = (bf16[32,3,8,128]{3,2,1,0:T(8,128)(2,1)}, f32[27,32,32]{2,1,0:T(8,128)}, f32[1,32]{1,0:T(1,128)}, f32[2,256]{1,0:T(2,128)}, f32[1,256]{1,0:T(1,...) custom-call(bf16[32,3,8,128]{3,2,1,0:T(8,128)(2,1)} %get-tuple-element.18.grad_in, ...), custom_call_target="tpu_custom_call" | custom-call | tf_op jit(solution)/shard_map/pallas_call | solution.py:525

commit v4 on v3

--- a/solution.py
+++ b/solution.py
@@ -45,8 +45,7 @@
             )
         )
     ]
-    for fetch in fetches:
-        fetch.start()
+    fetches[0].start()
     me_x, me_y, me_z = (lax.axis_index("gx"), lax.axis_index("gy"), lax.axis_index("gz"))
 
     def at(dx=0, dy=0, dz=0):
@@ -71,6 +70,14 @@
     barrier = pltpu.get_barrier_semaphore()
     for partner in partners:
         pl.semaphore_signal(barrier, inc=1, device_id=partner, device_id_type=MESH)
+    for fetch in fetches[1:]:
+        fetch.start()
+    sent = []
+
+    def launch(copies):
+        for copy in copies:
+            copy.start()
+        sent.extend(copies)
 
     def remote(src, dst, send, recv, device):
         return pltpu.make_async_remote_copy(
@@ -112,8 +119,7 @@
     def exchange(which, ext):
         near = side_copies(which, ext, True) + edge_copies(which, True)
         far = side_copies(which, ext, False) + edge_copies(which, False)
-        for copy in near + far:
-            copy.start()
+        launch(near + far)
         return near, far
 
     def pack_edges(which, ext):
@@ -130,18 +136,16 @@
         for y in range(EY):
             place_y, line = (0, CY - 1) if y == 0 else (2, 0) if y == EY - 1 else (1, y - 1)
             if place_y not in tiles_at:
-                tiles_at[place_y] = [
-                    edge_in[which, side, place_x, place_y].astype(jnp.float32)
-                    for side in (0, 1)
-                ]
-            before, after = tiles_at[place_y]
+                before, after = (
+                    edge_in[which, side, place_x, place_y].astype(jnp.float32) for side in (0, 1)
+                )
+                tiles_at[place_y] = jnp.where(lanes % 2 == 0, before, after)
             row = x * CY + line
             mid = ext[p, y]
             wide = mid.astype(jnp.float32)
-            low = jnp.where(lanes == 0, pltpu.roll(before, lax.rem(CZ - 2 * row, CZ), 1),
-                            pltpu.roll(wide, 1, 1))
-            high = jnp.where(lanes == CZ - 1, pltpu.roll(after, CZ - 2 - 2 * row, 1),
-                             pltpu.roll(wide, CZ - 1, 1))
+            rim = pltpu.roll(tiles_at[place_y], CZ - 1 - 2 * row, 1)
+            low = pltpu.roll(jnp.where(lanes == CZ - 1, rim, wide), 1, 1)
+            high = pltpu.roll(jnp.where(lanes == 0, rim, wide), CZ - 1, 1)
             out[p, y, 0:C] = low.astype(jnp.bfloat16)
             out[p, y, C : 2 * C] = mid
             out[p, y, 2 * C : 3 * C] = high.astype(jnp.bfloat16)
@@ -230,7 +234,7 @@
         cot[x] = jnp.swapaxes(cotangent[:, x].astype(jnp.float32), 0, 1)
 
     for copy in field_near:
-        copy.wait()
+        copy.wait_recv()
     build_near(0, field_ext, field_taps)
 
     depth = taps * C
@@ -263,11 +267,9 @@
 
     lax.fori_loop(0, CY // 2, forward_near, 0)
     for copy in field_far:
-        copy.wait()
+        copy.wait_recv()
     build_far(0, field_ext, field_taps)
     lax.fori_loop(0, CY // 2, forward_far, 0)
-    pack_edges(1, up_ext)
-    up_near, up_far = exchange(1, up_ext)
 
     def weigh(at_pair, carry):
         y = 2 * at_pair
@@ -318,15 +320,13 @@
         there = at(dz=k)
         reduce_z.append(remote(share.at[rows_at(there[2] * rows_z, rows_z)], from_z.at[k - 1],
                                rz_send.at[k - 1], rz_recv.at[k - 1], there))
+    launch(reduce_z)
+
+    pack_edges(1, up_ext)
+    up_near, up_far = exchange(1, up_ext)
+
     for copy in reduce_z:
-        copy.start()
-
-    for copy in up_near:
-        copy.wait()
-    build_near(1, up_ext, up_taps)
-
-    for copy in reduce_z:
-        copy.wait()
+        copy.wait_recv()
     mine = share[rows_at(me_z * rows_z, rows_z), :].astype(jnp.float32)
     for k in range(1, nz):
         mine = mine + from_z[k - 1].astype(jnp.float32)
@@ -337,9 +337,12 @@
         there = at(dx, dy)
         reduce_xy.append(remote(part_z.at[rows_at(there[1] * rows_y, rows_y)], from_xy.at[my_slot],
                                 rxy_send.at[k], rxy_recv.at[k], there))
-    for copy in reduce_xy:
-        copy.start()
+    launch(reduce_xy)
     from_xy[my_slot] = part_z[rows_at(me_y * rows_y, rows_y), :]
+
+    for copy in up_near:
+        copy.wait_recv()
+    build_near(1, up_ext, up_taps)
 
     def backward_near(at_pair, carry):
         y = 2 * at_pair
@@ -358,7 +361,7 @@
     lax.fori_loop(0, CY // 2, backward_near, 0)
 
     for copy in reduce_xy:
-        copy.wait()
+        copy.wait_recv()
     mine = from_xy[0].astype(jnp.float32)
     for k in range(1, nx * ny):
         mine = mine + from_xy[k].astype(jnp.float32)
@@ -368,16 +371,15 @@
         remote(total.at[own], total.at[own], g_send.at[k], g_recv.at[k], at(0, dy, dz))
         for k, (dy, dz) in enumerate(plane_yz)
     ]
-    for copy in gather:
-        copy.start()
+    launch(gather)
     for copy in up_far:
-        copy.wait()
+        copy.wait_recv()
     build_far(1, up_ext, up_taps)
     lax.fori_loop(0, CY // 2, backward_far, 0)
     for x in range(CX):
         grad[:, x] = jnp.swapaxes(turned_back[x], 0, 1).astype(jnp.bfloat16)
     for copy in gather:
-        copy.wait()
+        copy.wait_recv()
 
     last = taps - per * (tiles - 1)
     projected = jnp.zeros((C, CZ), jnp.float32)
@@ -424,6 +426,8 @@
     factor = jnp.minimum(1.0, lax.rsqrt(square_sum / entries + clip_eps))
     for j in range(tiles):
         grad_packed[j] = raws[j] * factor
+    for copy in sent:
+        copy.wait_send()
     grad_style_t[...] = style_raw * factor
     wide = lifted.shape[1]
     small = jnp.concatenate([offset_row, styles_grad], axis=1)

time: 33.3 us -> 33.1 us (level)
  no operation moved by 1% of the time
where the time goes in v4:
time: 33.1 us; the launch traced here: 32.9 us
  Pallas kernels  32.3 us (98%)
  between operations  0.64 us (2%)
    pallas_call x1, Pallas kernels, body(): pl.pallas_call(functools.partial(kernel_body, sizes), out_shape=[jax.Shap...  30.4 us
    pallas_call x1, Pallas kernels, body(): pl.pallas_call(hand_out, out_shape=[jax.ShapeDtypeStruct(field.shape, bf1...  1.91 us

profile of v4, /device:TPU:0, one launch (start us, length us, event | category | flops | bytes accessed | tf_op | source)
XLA Modules:
  0.0 32.9 jit_solution(4358108633314405383)
XLA Ops:
  0.6 30.4 %shard_map.144 = (bf16[32,3,8,128]{3,2,1,0:T(8,128)(2,1)}, f32[7,32,128]{2,1,0:T(8,128)}, f32[8,256]{1,0:T(8,128)}, f32[32,256]{1,0:T(8,128)}) custom-call(bf16[32,3,8,128]{3,2,1,0:T(8,128)(2,1)} %field_hbm.1, bf16[32,3,8,128]{3,2,1,0:T(8,128)(2,1)} %cotangent_hbm.1, f32[1,2]{1,0:T(1,128)} %bitcast.18, f32[2,256]{1,0:T(2,128)} %lift_weight_hbm.1, ...), custom_call_target="tpu_custom_call" | custom-call | tf_op jit(solution)/shard_map/pallas_call | solution.py:472
  31.0 1.9 %shard_map.145 = (bf16[32,3,8,128]{3,2,1,0:T(8,128)(2,1)}, f32[27,32,32]{2,1,0:T(8,128)}, f32[1,32]{1,0:T(1,128)}, f32[2,256]{1,0:T(2,128)}, f32[1,256]{1,0:T(1,...) custom-call(bf16[32,3,8,128]{3,2,1,0:T(8,128)(2,1)} %get-tuple-element.18.grad_in, ...), custom_call_target="tpu_custom_call" | custom-call | tf_op jit(solution)/shard_map/pallas_call | solution.py:529

commit v5 on v4

--- a/solution.py
+++ b/solution.py
@@ -24,7 +24,7 @@
     style_bias_hbm, kernel_hbm, offset_hbm,
     grad, grad_packed, grad_rows, grad_style_t,
     field, cotangent, cosmology, lift_weight, lift_bias, style_t, style_bias, kernel, offset,
-    fetch_sem, field_ext, up_ext, field_taps, up_taps, edge_out, edge_in, w_fwd, w_bwd, packed, cot, turned_back, held,
+    fetch_sem, field_ext, up_ext, field_taps, up_taps, edge_out, edge_in, w_fwd, w_bwd, packed, field_rows, cot, turned_back, held, up_turned,
     share, from_z, part_z, from_xy, total,
     xy_send, xy_recv, z_send, z_recv, rz_send, rz_recv, rxy_send, rxy_recv, g_send, g_recv,
 ):
@@ -134,13 +134,13 @@
     def build_taps(which, ext, out, p, place_x, x):
         tiles_at = {}
         for y in range(EY):
-            place_y, line = (0, CY - 1) if y == 0 else (2, 0) if y == EY - 1 else (1, y - 1)
+            place_y, source_y = (0, CY - 1) if y == 0 else (2, 0) if y == EY - 1 else (1, y - 1)
             if place_y not in tiles_at:
                 before, after = (
                     edge_in[which, side, place_x, place_y].astype(jnp.float32) for side in (0, 1)
                 )
                 tiles_at[place_y] = jnp.where(lanes % 2 == 0, before, after)
-            row = x * CY + line
+            row = x * CY + source_y
             mid = ext[p, y]
             wide = mid.astype(jnp.float32)
             rim = pltpu.roll(tiles_at[place_y], CZ - 1 - 2 * row, 1)
@@ -178,10 +178,14 @@
                 results[p - a] = term if results[p - a] is None else results[p - a] + term
         return results
 
+    def line(x, y):
+        return pl.ds(x * CY + y, C, stride=CX * CY)
+
     fetches[0].wait()
+    field_rows[...] = field[...].astype(jnp.float32).reshape(C * CX * CY, CZ)
     for x in range(CX):
-        turned_x = jnp.swapaxes(field[:, x].astype(jnp.float32), 0, 1)
-        field_ext[x + 1, 1 : CY + 1] = turned_x.astype(jnp.bfloat16)
+        for y in range(CY):
+            field_ext[x + 1, y + 1] = field_rows[line(x, y), :].astype(jnp.bfloat16)
     pack_edges(0, field_ext)
     pl.semaphore_wait(barrier, len(partners))
     field_near, field_far = exchange(0, field_ext)
@@ -230,8 +234,7 @@
             [turned[t] for t in taken], axis=1
         ).astype(jnp.bfloat16)
     offset_column = to_column(offset[...])
-    for x in range(CX):
-        cot[x] = jnp.swapaxes(cotangent[:, x].astype(jnp.float32), 0, 1)
+    cot[...] = cotangent[...].astype(jnp.float32).reshape(C * CX * CY, CZ)
 
     for copy in field_near:
         copy.wait_recv()
@@ -242,7 +245,7 @@
     edge_x = sorted({0, CX - 1})
 
     def finish(x, y, sums):
-        above = jnp.concatenate([cot[x, y], cot[x, y + 1]], axis=1)
+        above = jnp.concatenate([cot[line(x, y), :], cot[line(x, y + 1), :]], axis=1)
         upstream = (above * silu_slope(sums + offset_column)).astype(jnp.bfloat16)
         up_ext[x + 1, y + 1] = upstream[:, :CZ]
         up_ext[x + 1, y + 2] = upstream[:, CZ:]
@@ -271,31 +274,36 @@
     build_far(0, field_ext, field_taps)
     lax.fori_loop(0, CY // 2, forward_far, 0)
 
-    def weigh(at_pair, carry):
-        y = 2 * at_pair
-        sums, offsets = list(carry[:3]), carry[3]
-        ups = []
-        for x in range(CX):
-            upstream = jnp.concatenate([up_ext[x + 1, y + 1], up_ext[x + 1, y + 2]], axis=1)
-            wide = upstream.astype(jnp.float32)
-            offsets = offsets + wide[:, :CZ] + wide[:, CZ:]
-            ups.append(upstream)
-        for p in range(CX + 2):
-            taken = [a for a in range(3) if 0 <= p - a < CX]
-            product = lax.dot_general(
-                jnp.concatenate([ups[p - a] for a in taken], axis=0),
-                columns(field_taps, p, y), (((1,), (1,)), ((), ())),
-                preferred_element_type=jnp.float32,
-            )
-            for k, a in enumerate(taken):
-                sums[a] = sums[a] + product[k * C : (k + 1) * C]
-        return (*sums, offsets)
-
-    *sums, offsets = lax.fori_loop(
-        0, CY // 2, weigh,
-        (jnp.zeros((C, 9 * C), jnp.float32),) * 3 + (jnp.zeros((C, CZ), jnp.float32),),
+    offsets = jnp.zeros((C, CZ), jnp.float32)
+    blank = [jnp.zeros((C, CZ), jnp.float32)] * (per - CX)
+    for y in range(CY):
+        ups = [up_ext[x + 1, y + 1].astype(jnp.float32) for x in range(CX)]
+        for up in ups:
+            offsets = offsets + up
+        up_turned[y * CZ : (y + 1) * CZ, :] = jnp.concatenate(ups + blank, axis=0).T.astype(
+            jnp.bfloat16
+        )
+    block = lax.div(lax.broadcasted_iota(jnp.int32, (9 * C, CZ), 1), C)
+    products = []
+    for p in range(CX + 2):
+        streamed = jnp.concatenate(
+            [field_taps[p, y : y + 3].reshape(9 * C, CZ) for y in range(CY)], axis=1
+        )
+        products.append(jnp.dot(streamed, up_turned[...], preferred_element_type=jnp.float32))
+    merged = jnp.zeros((9 * C, CZ), jnp.float32)
+    for a in range(3):
+        chosen = products[a]
+        for x in range(1, CX):
+            chosen = jnp.where(block == x, products[a + x], chosen)
+        shift = CZ // 2
+        while shift >= C:
+            chosen = chosen + pltpu.roll(chosen, shift, 1)
+            shift //= 2
+        merged = jnp.where(block == a, chosen, merged)
+    flats = [merged[k : min(k + CZ, 9 * C)].T for k in range(0, 9 * C, CZ)]
+    sums = jnp.concatenate(
+        [flat[a * C : (a + 1) * C] for a in range(3) for flat in flats], axis=1
     )
-    sums = jnp.concatenate(sums, axis=1)
     offset_sum = jnp.sum(offsets, axis=1, keepdims=True)
     for j in range(share.shape[0] // C):
         if (j + 1) * CZ <= depth:
@@ -354,8 +362,8 @@
         y = 2 * at_pair
         results = [held[x, at_pair] for x in range(CX)]
         for x, sums in enumerate(convolve(w_bwd, up_taps, y, far_planes, results)):
-            turned_back[x, y] = sums[:, :CZ]
-            turned_back[x, y + 1] = sums[:, CZ:]
+            turned_back[line(x, y), :] = sums[:, :CZ]
+            turned_back[line(x, y + 1), :] = sums[:, CZ:]
         return carry
 
     lax.fori_loop(0, CY // 2, backward_near, 0)
@@ -376,8 +384,7 @@
         copy.wait_recv()
     build_far(1, up_ext, up_taps)
     lax.fori_loop(0, CY // 2, backward_far, 0)
-    for x in range(CX):
-        grad[:, x] = jnp.swapaxes(turned_back[x], 0, 1).astype(jnp.bfloat16)
+    grad[...] = turned_back[...].reshape(grad.shape).astype(jnp.bfloat16)
     for copy in gather:
         copy.wait_recv()
 
@@ -499,9 +506,11 @@
             pltpu.VMEM((3 * C, 9 * C), bf16),
             pltpu.VMEM((3 * C, 9 * C), bf16),
             pltpu.VMEM((tiles, C, CZ), f32),
-            pltpu.VMEM((CX, CY, C, CZ), f32),
-            pltpu.VMEM((CX, CY, C, CZ), f32),
+            pltpu.VMEM((C * CX * CY, CZ), f32),
+            pltpu.VMEM((C * CX * CY, CZ), f32),
+            pltpu.VMEM((C * CX * CY, CZ), f32),
             pltpu.VMEM((CX, CY // 2, C, 2 * CZ), f32),
+            pltpu.VMEM((CY * CZ, CZ), bf16),
             pltpu.VMEM((rows, CZ), bf16),
             pltpu.VMEM((nz - 1, rows // nz, CZ), bf16),
             pltpu.VMEM((rows // nz, CZ), bf16),

time: 33.1 us -> 33 us (level)
  no operation moved by 1% of the time
where the time goes in v5:
time: 33 us; the launch traced here: 32.8 us
  Pallas kernels  32.2 us (98%)
  between operations  0.64 us (2%)
    pallas_call x1, Pallas kernels, body(): pl.pallas_call(functools.partial(kernel_body, sizes), out_shape=[jax.Shap...  30.3 us
    pallas_call x1, Pallas kernels, body(): pl.pallas_call(hand_out, out_shape=[jax.ShapeDtypeStruct(field.shape, bf1...  1.91 us

profile of v5, /device:TPU:0, one launch (start us, length us, event | category | flops | bytes accessed | tf_op | source)
XLA Modules:
  0.0 32.8 jit_solution(7310012512081319802)
XLA Ops:
  0.6 30.3 %shard_map.144 = (bf16[32,3,8,128]{3,2,1,0:T(8,128)(2,1)}, f32[7,32,128]{2,1,0:T(8,128)}, f32[8,256]{1,0:T(8,128)}, f32[32,256]{1,0:T(8,128)}) custom-call(bf16[32,3,8,128]{3,2,1,0:T(8,128)(2,1)} %field_hbm.1, bf16[32,3,8,128]{3,2,1,0:T(8,128)(2,1)} %cotangent_hbm.1, f32[1,2]{1,0:T(1,128)} %bitcast.18, f32[2,256]{1,0:T(2,128)} %lift_weight_hbm.1, ...), custom_call_target="tpu_custom_call" | custom-call | tf_op jit(solution)/shard_map/pallas_call | solution.py:479
  30.9 1.9 %shard_map.145 = (bf16[32,3,8,128]{3,2,1,0:T(8,128)(2,1)}, f32[27,32,32]{2,1,0:T(8,128)}, f32[1,32]{1,0:T(1,128)}, f32[2,256]{1,0:T(2,128)}, f32[1,256]{1,0:T(1,...) custom-call(bf16[32,3,8,128]{3,2,1,0:T(8,128)(2,1)} %get-tuple-element.18.grad_in, ...), custom_call_target="tpu_custom_call" | custom-call | tf_op jit(solution)/shard_map/pallas_call | solution.py:538

commit v6 on v5

--- a/solution.py
+++ b/solution.py
@@ -119,7 +119,7 @@
     def exchange(which, ext):
         near = side_copies(which, ext, True) + edge_copies(which, True)
         far = side_copies(which, ext, False) + edge_copies(which, False)
-        launch(near + far)
+        launch(far + near)
         return near, far
 
     def pack_edges(which, ext):

time: 33 us -> 33.4 us (1.012)
  Pallas kernels: 32.2 us -> 32.6 us
    pallas_call x1, Pallas kernels: 30.3 us -> 30.7 us  [body(): pl.pallas_call(functools.partial(kernel_body, sizes), out_shape=[jax.Shap...]
where the time goes in v6:
time: 33.4 us; the launch traced here: 33.3 us
  Pallas kernels  32.6 us (98%)
  between operations  0.64 us (2%)
    pallas_call x1, Pallas kernels, body(): pl.pallas_call(functools.partial(kernel_body, sizes), out_shape=[jax.Shap...  30.7 us
    pallas_call x1, Pallas kernels, body(): pl.pallas_call(hand_out, out_shape=[jax.ShapeDtypeStruct(field.shape, bf1...  1.91 us

profile of v6, /device:TPU:0, one launch (start us, length us, event | category | flops | bytes accessed | tf_op | source)
XLA Modules:
  0.0 33.3 jit_solution(10020776372391850597)
XLA Ops:
  0.6 30.7 %shard_map.144 = (bf16[32,3,8,128]{3,2,1,0:T(8,128)(2,1)}, f32[7,32,128]{2,1,0:T(8,128)}, f32[8,256]{1,0:T(8,128)}, f32[32,256]{1,0:T(8,128)}) custom-call(bf16[32,3,8,128]{3,2,1,0:T(8,128)(2,1)} %field_hbm.1, bf16[32,3,8,128]{3,2,1,0:T(8,128)(2,1)} %cotangent_hbm.1, f32[1,2]{1,0:T(1,128)} %bitcast.18, f32[2,256]{1,0:T(2,128)} %lift_weight_hbm.1, ...), custom_call_target="tpu_custom_call" | custom-call | tf_op jit(solution)/shard_map/pallas_call | solution.py:479
  31.4 1.9 %shard_map.145 = (bf16[32,3,8,128]{3,2,1,0:T(8,128)(2,1)}, f32[27,32,32]{2,1,0:T(8,128)}, f32[1,32]{1,0:T(1,128)}, f32[2,256]{1,0:T(2,128)}, f32[1,256]{1,0:T(1,...) custom-call(bf16[32,3,8,128]{3,2,1,0:T(8,128)(2,1)} %get-tuple-element.18.grad_in, ...), custom_call_target="tpu_custom_call" | custom-call | tf_op jit(solution)/shard_map/pallas_call | solution.py:538
